TPU v7x, 1024 devices: a whole 4x4x32 slice. The times are simulated.
1024 devices in a mesh: feat: 64 (over z, core), dp: 16 (over x, y).
Axes of the slice: x: 4, y: 4, z: 32, core: 2. Of those that a mesh axis runs over, the one named last changes fastest.
Arguments:
- features: bfloat16 [16, 1024, 2048], P('dp', 'feat'), may hold values from -6 to 6
- neigh_lists: int32 [16, 10, 1024], P('dp'), may hold values from 0 to 2047
- w1_self: bfloat16 [1024, 512], P('feat'), may hold values from -0.125 to 0.125
- w1_neigh: bfloat16 [1024, 512], P('feat'), may hold values from -0.125 to 0.125
- w2_self: bfloat16 [512, 512], replicated, may hold values from -0.1875 to 0.1875
- w2_neigh: bfloat16 [512, 512], replicated, may hold values from -0.1875 to 0.1875
- send_rows: int32 [16, 64, 16, 8], P('dp', 'feat'), may hold values from 0 to 15
- send_count: int32 [16, 64, 16], P('dp', 'feat'), may hold values from 1 to 8, as said below
- recv_target: int32 [16, 64, 16, 8], P('dp', 'feat'), may hold values from 0 to 15
- out_grad: bfloat16 [16, 64, 16, 512], P('dp', 'feat'), may hold values from -6 to 6
Outputs:
- layer_out: bfloat16 [16, 64, 16, 512], P('dp', 'feat')
- grad_w1_self: float32 [16, 1024, 512], P('dp', 'feat')
- grad_w1_neigh: float32 [16, 1024, 512], P('dp', 'feat')
Inputs may be any that keep to these rules, and one draw needn't show every extreme that they name: `send_count`: for each feat index one data index, drawn from the seed, receives 8 live slots from every data peer; every other count is at most 4. `recv_target`: slots at or beyond the sending device's count carry nothing.
All inputs are finite; a program needn't handle non-finite values.
Results may differ from a plain program's by a relative error of at most 0.0277.
Values may be sent and summed in bfloat16 or wider, within the bound.
A program may use at most 32 MiB of HBM per device.

v0:
```python
import jax
import jax.numpy as jnp
from jax import lax
from jax.sharding import PartitionSpec as P

K1 = 10


def on_device(
    features,
    neigh_lists,
    w1_self,
    w1_neigh,
    w2_self,
    w2_neigh,
    send_rows,
    send_count,
    recv_target,
    out_grad,
):
    columns = features[0]
    neighbour_lists = neigh_lists[0]
    group_rows = neighbour_lists.shape[1]
    self_cols = columns[:, :group_rows]
    gathered = jnp.take(columns, neighbour_lists, axis=1)
    mean_cols = (jnp.sum(gathered, axis=1, dtype=jnp.float32) / K1).astype(jnp.bfloat16)
    feat_count = lax.axis_size("feat")
    rows_dev = group_rows // feat_count
    width = w1_self.shape[1]
    contract = (((0,), (0,)), ((), ()))
    part_self = self_cols
    part_mean = mean_cols
    term = lax.dot_general(part_self, w1_self, contract, preferred_element_type=jnp.float32)
    preact = lax.psum_scatter(
        term + lax.dot_general(part_mean, w1_neigh, contract, preferred_element_type=jnp.float32),
        "feat",
        scatter_dimension=0,
        tiled=True,
    )
    hidden = jnp.maximum(preact, 0.0).astype(jnp.bfloat16)
    dp_count = lax.axis_size("dp")
    rows_out = send_rows[0, 0]
    slot_count = rows_out.shape[1]
    outgoing = jnp.take(hidden, rows_out, axis=0)
    counts_out = send_count[0, 0].astype(jnp.bfloat16).reshape(dp_count, 1)
    incoming, counts_in = (
        lax.all_to_all(outgoing, "dp", split_axis=0, concat_axis=0, tiled=True),
        lax.all_to_all(counts_out, "dp", split_axis=0, concat_axis=0, tiled=True),
    )
    slot_ids = lax.broadcasted_iota(jnp.int32, (dp_count, slot_count), 1)
    usable = slot_ids < counts_in.astype(jnp.int32)
    targets = recv_target[0, 0]
    row_ids = lax.broadcasted_iota(jnp.int32, (rows_dev, dp_count * slot_count), 0)
    chosen = (row_ids == targets.reshape(1, -1)) & usable.reshape(1, -1)
    onehot = chosen.astype(jnp.bfloat16)
    neigh_sum = jnp.dot(
        onehot, incoming.reshape(dp_count * slot_count, width), preferred_element_type=jnp.float32
    )
    degree = jnp.sum(chosen.astype(jnp.float32), axis=1, keepdims=True)
    mean_two = ((hidden.astype(jnp.float32) + neigh_sum) / (1.0 + degree)).astype(jnp.bfloat16)
    layer_out = jnp.dot(hidden, w2_self, preferred_element_type=jnp.float32)
    layer_out = (
        layer_out + jnp.dot(mean_two, w2_neigh, preferred_element_type=jnp.float32)
    ).astype(jnp.bfloat16)
    upstream = out_grad[0, 0]
    transposed = (((1,), (1,)), ((), ()))
    grad_self = lax.dot_general(upstream, w2_self, transposed, preferred_element_type=jnp.float32)
    grad_mean = lax.dot_general(
        upstream, w2_neigh, transposed, preferred_element_type=jnp.float32
    ) / (1.0 + degree)
    returning = jnp.where(usable[..., None], jnp.take(grad_mean, targets, axis=0), 0.0)
    arrived = lax.all_to_all(
        returning.astype(jnp.bfloat16), "dp", split_axis=0, concat_axis=0, tiled=True
    ).astype(returning.dtype)
    own_table = (row_ids == rows_out.reshape(1, -1)).astype(jnp.float32)
    from_peers = jnp.dot(
        own_table, arrived.reshape(dp_count * slot_count, width), precision=lax.Precision.HIGHEST
    )
    grad_hidden = grad_self + grad_mean + from_peers
    grad_pre = jnp.where(preact > 0, grad_hidden, 0.0).astype(jnp.bfloat16)
    block_rows = lax.all_gather(grad_pre, "feat", axis=0, tiled=True)
    part_self = self_cols
    part_mean = mean_cols
    first = jnp.dot(part_self, block_rows, preferred_element_type=jnp.float32)
    second = jnp.dot(part_mean, block_rows, preferred_element_type=jnp.float32)
    return (layer_out[None, None], first[None], second[None])


def solution(mesh):
    in_specs = (
        P("dp", "feat", None),
        P("dp", None, None),
        P("feat", None),
        P("feat", None),
        P(),
        P(),
        P("dp", "feat", None, None),
        P("dp", "feat", None),
        P("dp", "feat", None, None),
        P("dp", "feat", None, None),
    )
    out_specs = (P("dp", "feat", None, None), P("dp", "feat", None), P("dp", "feat", None))
    return jax.shard_map(
        on_device, mesh=mesh, in_specs=in_specs, out_specs=out_specs, check_vma=False
    )
```

profile of v0, /device:TPU:1, one launch (start us, length us, event | category | flops | bytes accessed | tf_op | source)
XLA Modules:
  0.0 419.7 jit_solution(11830789796218541332)
XLA Ops:
  7.2 0.9 compare_select_fusion
  8.1 0.8 compare_and_fusion
  8.9 1.1 copy.43
  10.1 36.4 %gather_fusion = bf16[10240,16]{1,0:T(8,128)(2,1)} fusion(bf16[16,2048]{0,1:T(8,128)(2,1)S(1)} %bitcast.68, s32[10240]{0:T(1024)S(1)} %broadcast_clamp_fusion), kind=kCustom, calls=%fused_computation | custom fusion | bytes 696320 | tf_op jit(solution)/shard_map/jit(_take)/gather | solution.py:25
  46.9 4.2 %convert_reduce_fusion = f32[1024,16]{1,0:T(8,128)S(1)} fusion(bf16[10,1024,16]{2,1,0:T(8,128)(2,1)} %bitcast.71, pred[10,1024]{1,0:T(8,128)(4,1)S(1)} %compare_and_fusion), kind=kLoop, calls=%fused_computation.3 | loop fusion | flops 475136 | bytes 403456 | tf_op jit(solution)/shard_map/reduce_sum | solution.py:26
  51.2 1.8 convolution_add_fusion
  53.0 0.7 copy.45
  53.7 7.6 %all-to-all-start = ((bf16[16,1,1]{2,1,0:T(2,128)(2,1)}), bf16[16,1,1]{2,1,0:T(2,128)(2,1)S(1)}, u32[]{:S(2)}, u32[]{:S(2)}) async-start(bf16[16,1,1]{2,1,0:T(2,128)(2,1)} %copy.45), calls=%async_computation.1 | async-start | bytes 16384 | tf_op jit(solution)/shard_map/all_to_all | solution.py:48
  61.9 5.7 %all-to-all-done = bf16[16,1,1]{2,1,0:T(2,128)(2,1)S(1)} async-done(((bf16[16,1,1]{2,1,0:T(2,128)(2,1)}), bf16[16,1,1]{2,1,0:T(2,128)(2,1)S(1)}, u32[]{:S(2)}, u32[]{:S(2)}) %all-to-all-start) | async-done | bytes 64 | tf_op jit(solution)/shard_map/all_to_all | solution.py:48
  68.5 0.8 gather_fusion.2
  69.3 0.8 fusion.7
  70.1 3.5 all-to-all-start.2
  73.9 6.3 %all-to-all-done.2 = bf16[16,8,512]{2,1,0:T(8,128)(2,1)S(1)} async-done(((bf16[16,8,512]{2,1,0:T(8,128)(2,1)}), bf16[16,8,512]{2,1,0:T(8,128)(2,1)S(1)}, u32[]{:S(2)}, u32[]{:S(2)}) %all-to-all-start.2) | async-done | bytes 131104 | tf_op jit(solution)/shard_map/all_to_all | solution.py:72
  80.2 189.8 %reduce-scatter.2.cloned.1.call-done = f32[16,512]{1,0:T(8,128)} async-done(((f32[1024,512]{1,0:T(8,128)}), f32[16,512]{1,0:T(8,128)}) %reduce-scatter.2.cloned.1.call-update) | async-done | bytes 32784 | tf_op jit(solution)/shard_map/reduce_scatter | solution.py:34
  270.1 1.5 fusion.3
  271.9 0.8 maximum_convert_fusion
  272.6 0.8 gather_fusion.1
  273.5 0.7 bitcast_select_fusion.1
  274.2 6.4 %all-to-all-start.1 = ((bf16[16,8,512]{2,1,0:T(8,128)(2,1)}), bf16[16,8,512]{2,1,0:T(8,128)(2,1)S(1)}, u32[]{:S(2)}, u32[]{:S(2)}) async-start(bf16[16,8,512]{2,1,0:T(8,128)(2,1)} %bitcast_select_fusion.1), calls=%async_computation.2 | async-start | bytes 262144 | tf_op jit(solution)/shard_map/all_to_all | solution.py:47
  280.8 6.5 %all-to-all-done.1 = bf16[16,8,512]{2,1,0:T(8,128)(2,1)S(1)} async-done(((bf16[16,8,512]{2,1,0:T(8,128)(2,1)}), bf16[16,8,512]{2,1,0:T(8,128)(2,1)S(1)}, u32[]{:S(2)}, u32[]{:S(2)}) %all-to-all-start.1) | async-done | bytes 131104 | tf_op jit(solution)/shard_map/all_to_all | solution.py:47
  287.3 0.9 fusion.5
  288.2 120.4 %all-gather.2.cloned.1.call-done = bf16[1024,512]{1,0:T(8,128)(2,1)} async-done(((bf16[16,512]{1,0:T(8,128)(2,1)}), bf16[1024,512]{1,0:T(8,128)(2,1)}) %all-gather.2.cloned.1.call-update) | async-done | bytes 1048592 | tf_op jit(solution)/shard_map/all_gather | solution.py:81
  408.6 2.1 convolution_bitcast_fusion
  410.8 2.1 convolution_bitcast_fusion.1
  (47 shorter events, 2.7 us)
Async XLA Ops:
  7.2 66.5 %copy-start = (bf16[512,512]{1,0:T(8,128)(2,1)S(1)}, bf16[512,512]{1,0:T(8,128)(2,1)}, u32[]{:S(2)}) copy-start(bf16[512,512]{1,0:T(8,128)(2,1)} %param.14) | copy-start | bytes 1572868
  7.2 262.9 %reduce-scatter.2.cloned.1.call-start = ((), (), s32[]{:S(2)}) async-start(), calls=%async_computation.4 | async-start | bytes 2129920 | tf_op jit(solution)/shard_map/reduce_scatter | solution.py:34
  8.9 37.6 %copy-start.5 = (bf16[16,512]{1,0:T(8,128)(2,1)S(1)}, bf16[16,512]{1,0:T(8,128)(2,1)}, u32[]{:S(2)}) copy-start(bf16[16,512]{1,0:T(8,128)(2,1)} %param.12) | copy-start | bytes 49156
  46.5 4.6 %copy-start.6 = (bf16[16,512]{1,0:T(8,128)(2,1)S(1)}, bf16[16,512]{1,0:T(8,128)(2,1)}, u32[]{:S(2)}) copy-start(bf16[16,512]{1,0:T(8,128)(2,1)} %param.13) | copy-start | bytes 49156
  51.1 1.8 copy-start.7
  51.1 10.1 %copy-start.3 = (s32[1,1,16,8]{2,3,1,0:T(8,128)S(1)}, s32[1,1,16,8]{2,3,1,0:T(8,128)}, u32[]{:S(2)}) copy-start(s32[1,1,16,8]{2,3,1,0:T(8,128)} %param.18) | copy-start | bytes 1540
  51.1 10.6 %copy-start.4 = (s32[1,1,16,8]{2,3,1,0:T(8,128)S(1)}, s32[1,1,16,8]{2,3,1,0:T(8,128)}, u32[]{:S(2)}) copy-start(s32[1,1,16,8]{2,3,1,0:T(8,128)} %param.16) | copy-start | bytes 1540
  51.1 17.1 %copy-start.1 = (bf16[512,512]{1,0:T(8,128)(2,1)S(1)}, bf16[512,512]{1,0:T(8,128)(2,1)}, u32[]{:S(2)}) copy-start(bf16[512,512]{1,0:T(8,128)(2,1)} %param.15) | copy-start | bytes 1572868
  51.2 17.1 %copy-start.2 = (bf16[1,1,16,512]{3,2,1,0:T(8,128)(2,1)S(1)}, bf16[1,1,16,512]{3,2,1,0:T(8,128)(2,1)}, u32[]{:S(2)}) copy-start(bf16[1,1,16,512]{3,2,1,0:T(8,128)(2,1)} %param.19) | copy-start | bytes 49156
  53.7 13.9 %all-to-all-start = ((bf16[16,1,1]{2,1,0:T(2,128)(2,1)}), bf16[16,1,1]{2,1,0:T(2,128)(2,1)S(1)}, u32[]{:S(2)}, u32[]{:S(2)}) async-start(bf16[16,1,1]{2,1,0:T(2,128)(2,1)} %copy.45), calls=%async_computation.1 | async-start | bytes 16384 | tf_op jit(solution)/shard_map/all_to_all | solution.py:48
  70.1 10.1 %all-to-all-start.2 = ((bf16[16,8,512]{2,1,0:T(8,128)(2,1)}), bf16[16,8,512]{2,1,0:T(8,128)(2,1)S(1)}, u32[]{:S(2)}, u32[]{:S(2)}) async-start(bf16[16,8,512]{2,1,0:T(8,128)(2,1)} %fusion.7), calls=%async_computation.3 | async-start | bytes 262144 | tf_op jit(solution)/shard_map/all_to_all | solution.py:72
  73.6 335.0 %all-gather.2.cloned.1.call-start = ((), (), s32[]{:S(2)}) async-start(), calls=%async_computation.5 | async-start | bytes 1064960 | tf_op jit(solution)/shard_map/all_gather | solution.py:81
  274.2 13.1 %all-to-all-start.1 = ((bf16[16,8,512]{2,1,0:T(8,128)(2,1)}), bf16[16,8,512]{2,1,0:T(8,128)(2,1)S(1)}, u32[]{:S(2)}, u32[]{:S(2)}) async-start(bf16[16,8,512]{2,1,0:T(8,128)(2,1)} %bitcast_select_fusion.1), calls=%async_computation.2 | async-start | bytes 262144 | tf_op jit(solution)/shard_map/all_to_all | solution.py:47
Sparse Core Ops, SparseCore 0:
  53.1 216.9 reduce-scatter.1
  273.7 134.8 all-gather.1
where the time goes:
time: 420 us
  waiting for transfers between devices  329 us (78%)
  local copies, waits for them, and re-layouts  40.8 us (10%)
  starting transfers between devices  17.6 us (4%)
  between operations  14.3 us (3%)
  matrix products  9.41 us (2%)
  other arithmetic  8.79 us (2%)
    reduce_scatter x1, waiting for transfers between devices, on_device(): lax.psum_scatter(term + lax.dot_general(part_mean, w1_neigh, contract, pr...  190 us
    all_gather x1, waiting for transfers between devices, on_device(): block_rows = lax.all_gather(grad_pre, 'feat', axis=0, tiled=True)  120 us
    gather x1, local copies, waits for them, and re-layouts, on_device(): gathered = jnp.take(columns, neighbour_lists, axis=1)  36.4 us
  transfers between devices with their start and end apart: 5, of which 5 were waited for; matrix products, arithmetic and copies ran while one was open for 2% of the time, Pallas kernels for 0%

commit v1 on v0

v1 whole, which is shorter than its diff:
```python
import jax
import jax.numpy as jnp
from jax import lax
from jax.experimental import pallas as pl
from jax.experimental.pallas import tpu as pltpu
from jax.sharding import PartitionSpec as P

MESH = pl.DeviceIdType.MESH
K1 = 10
NZ = 32
NDP = 16
GROUPS = 8
LANES = 128
F32 = jnp.float32
BF16 = jnp.bfloat16

AG_PLAN = (
    (0, (8, -8, 4, -4, 1, -1, 2, -2)),
    (-4, (1, -1, 2)),
    (4, (1, -1, -2)),
    (-8, (8, 4, 1, -1, 2)),
    (8, (-4, 1, -1, -2)),
    (-12, (1, -1, 2)),
    (12, (1, -1, -2)),
    (16, (1, -1)),
)


def iota(shape, axis):
    return lax.broadcasted_iota(jnp.int32, shape, axis)


def dot(a, b):
    return jnp.dot(a, b, preferred_element_type=F32)


def dot_nt(a, b):
    return lax.dot_general(a, b, (((1,), (1,)), ((), ())), preferred_element_type=F32)


def kernel(
    feat_ref,
    lists_ref,
    w1s_ref,
    w1n_ref,
    w2s_ref,
    w2n_ref,
    rows_ref,
    count_ref,
    target_ref,
    og_ref,
    out_ref,
    gs_ref,
    gn_ref,
    xs,
    xp,
    xf,
    xt,
    xn,
    w,
    meta,
    gm_all,
    h_all,
    gp,
    part,
    part_in,
    res,
    res_in,
    w1f_s,
    w1f_r,
    far_s,
    far_r,
    near_s,
    near_r,
    wd_s,
    wd_r,
    meta_s,
    meta_r,
    gm_s,
    gm_r,
    h_s,
    h_r,
    ag_s,
    ag_r,
    d2d_s,
    d2d_r,
):
    f = lax.axis_index("feat")
    d = lax.axis_index("dp")
    z = f // 2
    q = lax.rem(f, 2)
    g = z // 4
    zeta = lax.rem(z, 4)
    partner = 2 * z + 1 - q

    def chip(zz):
        return {"feat": 2 * zz + q}

    def column(offset):
        return lax.rem(z + offset + NZ, NZ)

    def row_peer(i):
        return lax.rem(d + i, NDP)

    def copy(src, dst, send, recv, device):
        return pltpu.make_async_remote_copy(
            src_ref=src, dst_ref=dst, send_sem=send, recv_sem=recv, device_id=device, device_id_type=MESH
        )

    def signal(device):
        pl.semaphore_signal(barrier, inc=1, device_id=device, device_id_type=MESH)

    barrier = pltpu.get_barrier_semaphore()
    signal({"feat": partner})

    @pl.loop(1, NZ)
    def _(i):
        signal(chip(column(i)))

    @pl.loop(1, NDP)
    def _(i):
        signal({"dp": row_peer(i)})

    chunks = [feat_ref[:, LANES * i : LANES * (i + 1)].astype(F32) for i in range(16)]

    @pl.loop(0, GROUPS)
    def _(c):
        lanes = pl.ds(pl.multiple_of(c * LANES, LANES), LANES)

        block = lists_ref[:, lanes]
        total = jnp.zeros((16, LANES), F32)
        for k in range(K1):
            index = jnp.broadcast_to(block[k : k + 1], (16, LANES))
            low = lax.bitwise_and(index, 127)
            high = lax.shift_right_logical(index, 7)
            value = jnp.zeros((16, LANES), F32)
            for i in range(16):
                picked = jnp.take_along_axis(chunks[i], low, axis=1, mode="promise_in_bounds")
                value = jnp.where(high == i, picked, value)
            total += value
        xs[c, 0] = feat_ref[:, lanes]
        xs[c, 1] = (total / K1).astype(BF16)

    lane = iota((1, LANES), 1)
    slot = lax.rem(lane, 8)
    peer_rows = iota((NDP, LANES), 0) == iota((NDP, LANES), 1) // 8
    spread = (iota((8, LANES), 0) == lax.rem(iota((8, LANES), 1), 8)).astype(BF16)

    def flat(ref):
        wide = dot(ref[...].astype(F32).astype(BF16), spread)
        return jnp.sum(jnp.where(peer_rows, wide, 0.0), axis=0, keepdims=True)

    rows_own = flat(rows_ref)
    target_own = flat(target_ref)
    count_own = dot(count_ref[...].astype(F32).astype(BF16), peer_rows.astype(F32).astype(BF16))
    meta[d] = jnp.concatenate([rows_own, target_own, count_own, jnp.zeros((5, LANES), F32)], axis=0)

    pl.semaphore_wait(barrier, NZ - 1 + NDP - 1 + 1)

    xf[g] = xs[g]

    @pl.loop(1, GROUPS)
    def _(i):
        there = lax.rem(g + i, GROUPS)
        copy(xs.at[there], xf.at[g], far_s.at[i], far_r.at[g], chip(4 * there + zeta)).start()

    w_type = d // 8
    w_block = lax.rem(d // 2, 4)
    w_half = lax.rem(d, 2)
    w_lanes = pl.ds(pl.multiple_of(w_block * LANES, LANES), LANES)
    tile_rows = pl.ds(pl.multiple_of((lax.rem(zeta, 2) * 8 + g) * 16, 16), 16)
    sends_w = zeta // 2 == w_half

    @pl.when(sends_w & (w_type == 0))
    def _():
        w[d, tile_rows, :] = w1s_ref[:, w_lanes]

    @pl.when(sends_w & (w_type == 1))
    def _():
        w[d, tile_rows, :] = w1n_ref[:, w_lanes]

    def w_far(i):
        return copy(
            w.at[d, tile_rows, :], w.at[d, tile_rows, :], w1f_s.at[i], w1f_r.at[z], chip(column(i))
        )

    @pl.when(sends_w)
    def _():
        @pl.loop(1, NZ)
        def _(i):
            w_far(i).start()

    @pl.loop(1, NDP)
    def _(i):
        copy(meta.at[d], meta.at[d], meta_s.at[i], meta_r.at[d], {"dp": row_peer(i)}).start()

    swap_x = copy(xs, xp, d2d_s.at[0], d2d_r.at[0], {"feat": partner})
    swap_x.start()

    @pl.loop(1, NDP)
    def _(i):
        e = row_peer(i)
        copy(meta.at[e], meta.at[e], meta_s.at[i], meta_r.at[e], {"dp": e}).wait_recv()

    mine = iota((NDP, LANES), 1) // 8 == d
    same_slot = (lax.rem(iota((LANES, LANES), 0), 8) == lax.rem(iota((LANES, LANES), 1), 8)).astype(BF16)

    def from_peers(row):
        wide = dot(jnp.where(mine, meta[:, row, :], 0.0).astype(BF16), same_slot)
        return jnp.sum(jnp.where(peer_rows, wide, 0.0), axis=0, keepdims=True)

    rows_in = from_peers(0)
    target_in = from_peers(1)
    count_in = from_peers(2)
    slot_f = slot.astype(F32)
    base = (lane // 8 * 16).astype(F32)
    node = iota((16, LANES), 0).astype(F32)
    hits_in = jnp.where((target_own == node) & (slot_f < count_in), 1.0, 0.0)
    hits_out = jnp.where((rows_own == node) & (slot_f < count_own), 1.0, 0.0)
    everyone = iota((NDP * 16, LANES), 0).astype(F32)
    table_in = jnp.where(everyone == base + rows_in, 1.0, 0.0).astype(BF16)
    table_out = jnp.where(everyone == base + target_in, 1.0, 0.0).astype(BF16)
    mix_in = dot_nt(hits_in.astype(BF16), table_in).astype(BF16)
    mix_out = dot_nt(hits_out.astype(BF16), table_out).astype(BF16)
    degree = jnp.sum(hits_in, axis=1, keepdims=True)

    og = og_ref[...]
    grad_self = dot_nt(og, w2s_ref[...])
    grad_mean = dot_nt(og, w2n_ref[...]) / (1.0 + degree)
    gm_all[d] = grad_mean.astype(BF16)

    @pl.loop(1, NDP)
    def _(i):
        copy(gm_all.at[d], gm_all.at[d], gm_s.at[i], gm_r.at[d], {"dp": row_peer(i)}).start()

    swap_x.wait_recv()
    node_in = iota((1024, 512), 0)
    node_at = iota((1024, 512), 1)
    pick = jnp.where(node_in == 32 * (node_at // 16) + 16 * q + lax.rem(node_at, 16), 1.0, 0.0).astype(BF16)
    wide_rows = jnp.concatenate(
        [
            jnp.concatenate([buf[c, kind] for c in range(GROUPS)], axis=1)
            for buf in (xs, xp)
            for kind in (0, 1)
        ],
        axis=0,
    )
    x_cols = dot(wide_rows, pick).astype(BF16)

    @pl.loop(1, NDP)
    def _(i):
        e = row_peer(i)
        copy(gm_all.at[e], gm_all.at[e], gm_s.at[i], gm_r.at[e], {"dp": e}).wait_recv()

    back = dot(mix_out, gm_all[...].reshape(NDP * 16, 512))
    grad_hidden = grad_self + grad_mean + back

    @pl.loop(1, GROUPS)
    def _(i):
        there = lax.rem(g + i, GROUPS)
        copy(xf.at[there], xf.at[there], far_s.at[i], far_r.at[there], chip(4 * there + zeta)).wait_recv()

    for kind in (0, 1):
        turned = jnp.transpose(xf[:, kind].reshape(LANES, LANES).astype(F32)).astype(BF16)
        for i in range(4):
            xt[i, kind] = turned[32 * i : 32 * (i + 1)]
    xn[zeta] = xt[zeta]

    @pl.loop(1, 4)
    def _(i):
        there = lax.rem(zeta + i, 4)
        copy(xt.at[there], xn.at[zeta], near_s.at[i], near_r.at[zeta], chip(4 * g + there)).start()

    def w_source(i):
        from_zeta = 2 * w_half + i // 8
        from_g = lax.rem(i, 8)
        return 4 * from_g + from_zeta

    @pl.loop(0, 16)
    def _(i):
        source = w_source(i)
        at = pl.ds(pl.multiple_of(i * 16, 16), 16)

        @pl.when(source != z)
        def _():
            copy(w.at[d, at, :], w.at[d, at, :], w1f_s.at[0], w1f_r.at[source], chip(source)).wait_recv()

    @pl.loop(1, NDP)
    def _(i):
        copy(w.at[d], w.at[d], wd_s.at[i], wd_r.at[d], {"dp": row_peer(i)}).start()

    @pl.loop(1, 4)
    def _(i):
        there = lax.rem(zeta + i, 4)
        copy(xn.at[there], xn.at[there], near_s.at[i], near_r.at[there], chip(4 * g + there)).wait_recv()

    @pl.loop(1, NDP)
    def _(i):
        e = row_peer(i)
        copy(w.at[e], w.at[e], wd_s.at[i], wd_r.at[e], {"dp": e}).wait_recv()

    for block in range(4):
        total = jnp.zeros((32, LANES), F32)
        for kind in (0, 1):
            for half in (0, 1):
                x_part = jnp.concatenate([xn[2 * half, kind], xn[2 * half + 1, kind]], axis=1)
                total += dot(x_part, w[kind * 8 + block * 2 + half])
        part[0, :, LANES * block : LANES * (block + 1)] = total[:16]
        part[1, :, LANES * block : LANES * (block + 1)] = total[16:]

    swap_p = copy(part.at[1 - q], part_in, d2d_s.at[1], d2d_r.at[1], {"feat": partner})
    swap_p.start()
    swap_p.wait_recv()
    preact = part[q] + part_in[...]
    hidden = jnp.maximum(preact, 0.0).astype(BF16)
    gp[z] = jnp.where(preact > 0, grad_hidden, 0.0).astype(BF16)
    h_all[d] = hidden

    sent = []

    def pass_on(offset, targets):
        at = gp.at[column(offset)]
        for target in targets:
            c = copy(at, at, ag_s.at[len(sent)], ag_r.at[column(offset)], chip(column(target)))
            c.start()
            sent.append(c)

    def arrived(offset):
        at = gp.at[column(offset)]
        copy(at, at, ag_s.at[0], ag_r.at[column(offset)], chip(column(offset))).wait_recv()

    pass_on(*AG_PLAN[0])

    @pl.loop(1, NDP)
    def _(i):
        copy(h_all.at[d], h_all.at[d], h_s.at[i], h_r.at[d], {"dp": row_peer(i)}).start()

    for offset, targets in AG_PLAN[1:3]:
        arrived(offset)
        pass_on(offset, targets)

    @pl.loop(1, NDP)
    def _(i):
        e = row_peer(i)
        copy(h_all.at[e], h_all.at[e], h_s.at[i], h_r.at[e], {"dp": e}).wait_recv()

    neigh_sum = dot(mix_in, h_all[...].reshape(NDP * 16, 512))
    mean_two = ((hidden.astype(F32) + neigh_sum) / (1.0 + degree)).astype(BF16)
    out_ref[...] = (dot(hidden, w2s_ref[...]) + dot(mean_two, w2n_ref[...])).astype(BF16)

    for offset, targets in AG_PLAN[3:]:
        arrived(offset)
        pass_on(offset, targets)
    known = [offset % NZ for offset, _ in AG_PLAN]
    for offset in range(1, NZ):
        if offset not in known:
            arrived(offset)

    total = dot(x_cols, gp[...].reshape(NZ * 16, 512))
    res[...] = total
    swap_r = copy(res.at[32:64], res_in, d2d_s.at[2], d2d_r.at[2], {"feat": partner})
    swap_r.start()
    swap_r.wait_recv()
    gs_ref[...] = res[0:16] + res_in[0:16]
    gn_ref[...] = res[16:32] + res_in[16:32]

    for c in sent + [swap_x, swap_p, swap_r]:
        c.wait_send()

    @pl.loop(1, GROUPS)
    def _(i):
        there = lax.rem(g + i, GROUPS)
        copy(xs.at[there], xf.at[g], far_s.at[i], far_r.at[g], chip(4 * there + zeta)).wait_send()

    @pl.loop(1, 4)
    def _(i):
        there = lax.rem(zeta + i, 4)
        copy(xt.at[there], xn.at[zeta], near_s.at[i], near_r.at[zeta], chip(4 * g + there)).wait_send()

    @pl.when(sends_w)
    def _():
        @pl.loop(1, NZ)
        def _(i):
            w_far(i).wait_send()

    @pl.loop(1, NDP)
    def _(i):
        to = {"dp": row_peer(i)}
        copy(meta.at[d], meta.at[d], meta_s.at[i], meta_r.at[d], to).wait_send()
        copy(gm_all.at[d], gm_all.at[d], gm_s.at[i], gm_r.at[d], to).wait_send()
        copy(h_all.at[d], h_all.at[d], h_s.at[i], h_r.at[d], to).wait_send()
        copy(w.at[d], w.at[d], wd_s.at[i], wd_r.at[d], to).wait_send()


def on_device(
    features,
    neigh_lists,
    w1_self,
    w1_neigh,
    w2_self,
    w2_neigh,
    send_rows,
    send_count,
    recv_target,
    out_grad,
):
    dma = pltpu.SemaphoreType.DMA
    vmem = pl.BlockSpec(memory_space=pltpu.VMEM)
    layer_out, grad_self, grad_neigh = pl.pallas_call(
        kernel,
        out_shape=(
            jax.ShapeDtypeStruct((16, 512), BF16),
            jax.ShapeDtypeStruct((16, 512), F32),
            jax.ShapeDtypeStruct((16, 512), F32),
        ),
        in_specs=[vmem] * 10,
        out_specs=(vmem, vmem, vmem),
        scratch_shapes=[
            pltpu.VMEM((GROUPS, 2, 16, LANES), BF16),
            pltpu.VMEM((GROUPS, 2, 16, LANES), BF16),
            pltpu.VMEM((GROUPS, 2, 16, LANES), BF16),
            pltpu.VMEM((4, 2, 32, LANES), BF16),
            pltpu.VMEM((4, 2, 32, LANES), BF16),
            pltpu.VMEM((NDP, 256, LANES), BF16),
            pltpu.VMEM((NDP, 8, LANES), F32),
            pltpu.VMEM((NDP, 16, 512), BF16),
            pltpu.VMEM((NDP, 16, 512), BF16),
            pltpu.VMEM((NZ, 16, 512), BF16),
            pltpu.VMEM((2, 16, 512), F32),
            pltpu.VMEM((16, 512), F32),
            pltpu.VMEM((64, 512), F32),
            pltpu.VMEM((32, 512), F32),
            dma((NZ,)),
            dma((NZ,)),
            dma((GROUPS,)),
            dma((GROUPS,)),
            dma((4,)),
            dma((4,)),
            dma((NDP,)),
            dma((NDP,)),
            dma((NDP,)),
            dma((NDP,)),
            dma((NDP,)),
            dma((NDP,)),
            dma((NDP,)),
            dma((NDP,)),
            dma((NZ,)),
            dma((NZ,)),
            dma((3,)),
            dma((3,)),
        ],
        compiler_params=pltpu.CompilerParams(
            collective_id=0, has_side_effects=True, vmem_limit_bytes=40 * 1024 * 1024
        ),
    )(
        features[0],
        neigh_lists[0],
        w1_self,
        w1_neigh,
        w2_self,
        w2_neigh,
        send_rows[0, 0],
        send_count[0],
        recv_target[0, 0],
        out_grad[0, 0],
    )
    return layer_out[None, None], grad_self[None], grad_neigh[None]


def solution(mesh):
    in_specs = (
        P("dp", "feat", None),
        P("dp", None, None),
        P("feat", None),
        P("feat", None),
        P(),
        P(),
        P("dp", "feat", None, None),
        P("dp", "feat", None),
        P("dp", "feat", None, None),
        P("dp", "feat", None, None),
    )
    out_specs = (P("dp", "feat", None, None), P("dp", "feat", None), P("dp", "feat", None))
    return jax.shard_map(
        on_device, mesh=mesh, in_specs=in_specs, out_specs=out_specs, check_vma=False
    )
```

time: 420 us -> 94 us (0.22)
  waiting for transfers between devices: 329 us -> 0 us
  Pallas kernels: 0 us -> 86.8 us
  local copies, waits for them, and re-layouts: 40.8 us -> 6.17 us
  starting transfers between devices: 17.6 us -> 0 us
  between operations: 14.3 us -> 0.7 us
  matrix products: 9.41 us -> 0 us
  other arithmetic: 8.79 us -> 0 us
    reduce_scatter x1 -> x0, waiting for transfers between devices: 190 us -> none  [on_device(): lax.psum_scatter(term + lax.dot_general(part_mean, w1_neigh, contract, pr...]
    all_gather x1 -> x0, waiting for transfers between devices: 120 us -> none  [on_device(): block_rows = lax.all_gather(grad_pre, 'feat', axis=0, tiled=True)]
    pallas_call x0 -> x1, Pallas kernels: none -> 86.8 us  [on_device(): pl.pallas_call(kernel, out_shape=(jax.ShapeDtypeStruct((16, 512), BF16),...]
    gather x3 -> x0, local copies, waits for them, and re-layouts: 38 us -> none  [the longest x1 36.4 us: on_device(): gathered = jnp.take(columns, neighbour_lists, axis=1)]
    all_to_all x3 -> x0, waiting for transfers between devices: 18.6 us -> none  [the longest x1 6.52 us: on_device(): lax.all_to_all(outgoing, 'dp', split_axis=0, concat_axis=0, tiled=True)]
    all_to_all x3 -> x0, starting transfers between devices: 17.5 us -> none  [the longest x1 7.59 us: on_device(): lax.all_to_all(counts_out, 'dp', split_axis=0, concat_axis=0, tiled=True)]
    dot_general x9 -> x0, matrix products: 9.41 us -> none  [the longest x1 2.13 us: on_device(): first = jnp.dot(part_self, block_rows, preferred_element_type=jnp.float32)]
    unnamed x19 -> x22, local copies, waits for them, and re-layouts: 1.31 us -> 6.03 us
  transfers between devices with their start and end apart: 5 -> 0, of which waited for: 5 -> 0; matrix products, arithmetic and copies ran while one was open for 2% -> 0% of each run, Pallas kernels for 0% -> 0%
where the time goes in v1:
time: 94 us; the launch traced here: 93.7 us
  Pallas kernels  86.8 us (92%)
  local copies, waits for them, and re-layouts  6.17 us (7%)
    pallas_call x1, Pallas kernels, on_device(): pl.pallas_call(kernel, out_shape=(jax.ShapeDtypeStruct((16, 512), BF16),...  86.8 us
    unnamed x22, local copies, waits for them, and re-layouts  6.03 us

profile of v1, /device:TPU:1, one launch (start us, length us, event | category | flops | bytes accessed | tf_op | source)
XLA Modules:
  0.0 93.7 jit_solution(14826253955707751505)
XLA Ops:
  0.6 0.0 copy-start.7
  0.6 0.0 copy-start.8
  0.7 0.7 copy-done.7
  1.3 0.0 copy-start.2
  1.3 0.1 copy.13.rows_ref
  1.4 0.0 copy-done.8
  1.4 0.1 copy.14.target_ref
  1.5 0.0 copy-start.3
  1.5 0.0 copy-start.4
  1.5 0.0 copy-start.5
  1.5 0.8 copy.17
  2.3 0.0 copy-start.6
  2.3 0.0 copy-done.2
  2.3 0.0 copy-done.3
  2.3 0.0 copy-done.4
  2.3 0.0 copy-done.5
  2.3 0.6 copy-done.6
  2.9 0.0 copy-start
  3.0 1.0 %copy-done = bf16[512,512]{1,0:T(8,128)(2,1)S(1)} copy-done((bf16[512,512]{1,0:T(8,128)(2,1)S(1)}, bf16[512,512]{1,0:T(8,128)(2,1)}, u32[]{:S(2)}) %copy-start) | copy-done | bytes 524312
  4.0 1.0 %copy-done.1 = bf16[512,512]{1,0:T(8,128)(2,1)S(1)} copy-done((bf16[512,512]{1,0:T(8,128)(2,1)S(1)}, bf16[512,512]{1,0:T(8,128)(2,1)}, u32[]{:S(2)}) %copy-start.1) | copy-done | bytes 524312
  5.0 86.8 %shard_map.121 = (bf16[16,512]{1,0:T(8,128)(2,1)S(1)}, f32[16,512]{1,0:T(8,128)S(1)}, f32[16,512]{1,0:T(8,128)S(1)}) custom-call(bf16[16,2048]{1,0:T(8,128)(2,1)S(1)} %bitcast.12, s32[10,1024]{1,0:T(8,128)S(1)} %bitcast.11, bf16[16,512]{1,0:T(8,128)(2,1)S(1)} %copy-done.3, bf16[16,512]{1,0:T(8,128)(2,1)S(1)} %copy-done.4, bf16[512,512]{1,0:T(8,128)(2,1)S(1)} %copy-done, ...), custom_call_target="tpu_custom_call" | custom-call | tf_op jit(solution)/shard_map/pallas_call | solution.py:409
  91.8 0.6 copy.21
  92.4 0.6 copy.22
  93.0 0.6 copy.23
  (1 shorter events, 0.0 us)
Async XLA Ops:
  0.6 0.7 copy-start.7
  0.6 0.8 copy-start.8
  1.3 1.0 %copy-start.2 = (bf16[1,16,2048]{2,1,0:T(8,128)(2,1)S(1)}, bf16[1,16,2048]{2,1,0:T(8,128)(2,1)}, u32[]{:S(2)}) copy-start(bf16[1,16,2048]{2,1,0:T(8,128)(2,1)} %param.10) | copy-start | bytes 196612
  1.5 0.8 copy-start.3
  1.5 0.9 copy-start.4
  1.5 0.9 copy-start.5
  2.3 0.7 copy-start.6
  2.9 1.0 %copy-start = (bf16[512,512]{1,0:T(8,128)(2,1)S(1)}, bf16[512,512]{1,0:T(8,128)(2,1)}, u32[]{:S(2)}) copy-start(bf16[512,512]{1,0:T(8,128)(2,1)} %w2s_ref.1) | copy-start | bytes 1572868
  4.0 1.0 %copy-start.1 = (bf16[512,512]{1,0:T(8,128)(2,1)S(1)}, bf16[512,512]{1,0:T(8,128)(2,1)}, u32[]{:S(2)}) copy-start(bf16[512,512]{1,0:T(8,128)(2,1)} %w2n_ref.1) | copy-start | bytes 1572868

commit v2 on v1

v2 whole, which is shorter than its diff:
```python
import jax
import jax.numpy as jnp
from jax import lax
from jax.experimental import pallas as pl
from jax.experimental.pallas import tpu as pltpu
from jax.sharding import PartitionSpec as P

MESH = pl.DeviceIdType.MESH
K1 = 10
NZ = 32
NDP = 16
GROUPS = 8
LANES = 128
F32 = jnp.float32
BF16 = jnp.bfloat16

WINDOW_PLAN = (
    (0, (-8, 5, -5, 2, -2, 1, -1)),
    (5, (2, -2, 1, -1)),
    (-5, (2, -2, 1, -1)),
)


def place(offset):
    if offset <= -16:
        offset += NZ
    return offset + 7 if offset >= -7 else 16 - offset


def iota(shape, axis):
    return lax.broadcasted_iota(jnp.int32, shape, axis)


def dot(a, b):
    return jnp.dot(a, b, preferred_element_type=F32)


def dot_nt(a, b):
    return lax.dot_general(a, b, (((1,), (1,)), ((), ())), preferred_element_type=F32)


def kernel(
    feat_ref,
    lists_ref,
    w1s_ref,
    w1n_ref,
    w2s_hbm,
    w2n_hbm,
    rows_ref,
    count_ref,
    target_ref,
    og_ref,
    out_ref,
    gs_ref,
    gn_ref,
    w2s_ref,
    w2n_ref,
    xs,
    xp,
    tiles,
    slots,
    relay_up,
    relay_down,
    w,
    w_own,
    w_relay,
    meta,
    gm_all,
    h_all,
    gh_own,
    gh_relay,
    gh_opp,
    gp,
    part,
    part_in,
    res,
    res_in,
    local_s,
    x_s,
    x_r,
    relay_s,
    relay_r,
    wz_s,
    wz_r,
    wr_s,
    wr_r,
    wd_s,
    wd_r,
    meta_s,
    meta_r,
    gm_s,
    gm_r,
    h_s,
    h_r,
    gh_s,
    gh_r,
    gp_s,
    gp_r,
    d2d_s,
    d2d_r,
):
    f = lax.axis_index("feat")
    d = lax.axis_index("dp")
    z = f // 2
    q = lax.rem(f, 2)
    partner = {"feat": 2 * z + 1 - q}
    sends = []

    def chip(offset):
        return {"feat": 2 * lax.rem(z + offset + NZ, NZ) + q}

    def row_peer(i):
        return lax.rem(d + i, NDP)

    def copy(src, dst, send, recv, device):
        return pltpu.make_async_remote_copy(
            src_ref=src, dst_ref=dst, send_sem=send, recv_sem=recv, device_id=device, device_id_type=MESH
        )

    def send(src, dst, send_sem, recv_sem, device):
        c = copy(src, dst, send_sem, recv_sem, device)
        c.start()
        sends.append(c)
        return c

    def arrived(dst, recv_sem):
        copy(dst, dst, d2d_s.at[0], recv_sem, partner).wait_recv()

    def to_row(src, dst, send_sem, recv_sem):
        @pl.loop(1, NDP)
        def _(i):
            copy(src, dst, send_sem.at[i], recv_sem.at[d], {"dp": row_peer(i)}).start()

    def from_row(buf, recv_sem):
        @pl.loop(1, NDP)
        def _(i):
            e = row_peer(i)
            arrived(buf.at[e], recv_sem.at[e])

    barrier = pltpu.get_barrier_semaphore()

    def signal(device):
        pl.semaphore_signal(barrier, inc=1, device_id=device, device_id_type=MESH)

    for offset in range(8, 0, -1):
        signal(chip(offset))
        signal(chip(-offset))
    signal(partner)

    @pl.loop(1, NDP)
    def _(i):
        signal({"dp": row_peer(i)})

    get_w2s = pltpu.make_async_copy(w2s_hbm, w2s_ref, local_s.at[0])
    get_w2n = pltpu.make_async_copy(w2n_hbm, w2n_ref, local_s.at[1])
    get_w2s.start()
    get_w2n.start()

    chunks = [feat_ref[:, LANES * i : LANES * (i + 1)].astype(F32) for i in range(16)]

    @pl.loop(0, GROUPS)
    def _(c):
        lanes = pl.ds(pl.multiple_of(c * LANES, LANES), LANES)
        total = jnp.zeros((16, LANES), F32)
        for k in range(K1):
            index = jnp.broadcast_to(lists_ref[k, :, lanes], (16, LANES))
            low = lax.bitwise_and(index, 127)
            high = lax.shift_right_logical(index, 7)
            value = jnp.zeros((16, LANES), F32)
            for i in range(16):
                picked = jnp.take_along_axis(chunks[i], low, axis=1, mode="promise_in_bounds")
                value = jnp.where(high == i, picked, value)
            total += value
        xs[c, 0] = feat_ref[:, lanes]
        xs[c, 1] = (total / K1).astype(BF16)

    quarter = iota((16, LANES), 1) // 32

    @pl.loop(0, GROUPS)
    def _(c):
        far = lax.rem(c + 4, GROUPS)
        parts = [xs[c, 0], xs[c, 1], xs[far, 0], xs[far, 1]]
        parts = [p.astype(F32) for p in parts]
        for i in range(4):
            tile = jnp.zeros((16, LANES), F32)
            for k in range(4):
                shift = (32 * (k - i)) % LANES
                moved = pltpu.roll(parts[k], shift, 1) if shift else parts[k]
                tile = jnp.where(quarter == k, moved, tile)
            tiles[lax.rem(4 * c + i - z + NZ, NZ)] = tile.astype(BF16)

    slots[place(0)] = tiles[0]

    lane = iota((1, LANES), 1)
    slot = lax.rem(lane, 8)
    peer_rows = iota((NDP, LANES), 0) == iota((NDP, LANES), 1) // 8
    spread = peer_rows.astype(F32).astype(BF16)
    own_slot = iota((8, LANES), 0) == lax.rem(iota((8, LANES), 1), 8)

    def flat(ref):
        wide = dot(ref[...].astype(F32).astype(BF16), spread)
        return jnp.sum(jnp.where(own_slot, wide, 0.0), axis=0, keepdims=True)

    rows_own = flat(rows_ref)
    target_own = flat(target_ref)
    count_own = dot(count_ref[...].astype(F32).astype(BF16), spread)
    meta[d] = jnp.concatenate([rows_own, target_own, count_own, jnp.zeros((5, LANES), F32)], axis=0)

    piece = lax.rem(d, 8)
    w_lanes = pl.ds(pl.multiple_of(lax.rem(d, 4) * LANES, LANES), LANES)
    near_column = d < 8
    own_tile = jnp.where(piece < 4, w1s_ref[:, w_lanes].astype(F32), w1n_ref[:, w_lanes].astype(F32)).astype(BF16)
    w_own[...] = own_tile

    @pl.when(near_column)
    def _():
        w[d, pl.ds(16 * place(0), 16), :] = own_tile

    def w_at(offset):
        return w.at[d, pl.ds(16 * (place(offset) % 16), 16), :]

    pl.semaphore_wait(barrier, 16 + 1 + NDP - 1)

    send(tiles.at[pl.ds(9, 8)], relay_up, relay_s.at[0], relay_r.at[0], chip(8))
    send(tiles.at[pl.ds(17, 7)], relay_down, relay_s.at[1], relay_r.at[1], chip(-8))

    w_near = [t for k in range(8, 0, -1) for t in (-k, k) if t != 8]
    w_near_sends = [
        copy(w_own, w_at(-t), wz_s.at[n], wz_r.at[place(-t) % 16], chip(t)) for n, t in enumerate(w_near)
    ]
    w_up = copy(w_own, w_at(-8), wr_s.at[0], wz_r.at[place(-8) % 16], chip(8))
    w_down = copy(w_own, w_relay, wr_s.at[1], wr_r.at[0], chip(-8))
    w_far_sends = [
        copy(w_at(-8), w_at(-8 - t), wz_s.at[t - 1], wz_r.at[place(-8 - t) % 16], chip(t)) for t in range(8, 0, -1)
    ] + [
        copy(w_relay, w_at(8 + t), wz_s.at[7 + t], wz_r.at[place(8 + t) % 16], chip(-t)) for t in range(7, 0, -1)
    ]

    @pl.when(jnp.logical_not(near_column))
    def _():
        w_up.start()
        w_down.start()

    for k in range(8, 0, -1):
        for t in (k, -k):
            send(tiles.at[t % NZ], slots.at[place(-t)], x_s.at[t + 8], x_r.at[place(-t)], chip(t))

    @pl.when(near_column)
    def _():
        for c in w_near_sends:
            c.start()

    to_row(meta.at[d], meta.at[d], meta_s, meta_r)
    send(xs, xp, d2d_s.at[0], d2d_r.at[0], partner)

    from_row(meta, meta_r)
    mine = iota((NDP, LANES), 1) // 8 == d
    same_slot = (lax.rem(iota((LANES, LANES), 0), 8) == lax.rem(iota((LANES, LANES), 1), 8)).astype(BF16)

    def from_peers(row):
        wide = dot(jnp.where(mine, meta[:, row, :], 0.0).astype(BF16), same_slot)
        return jnp.sum(jnp.where(peer_rows, wide, 0.0), axis=0, keepdims=True)

    rows_in = from_peers(0)
    target_in = from_peers(1)
    count_in = from_peers(2)
    slot_f = slot.astype(F32)
    base = (lane // 8 * 16).astype(F32)
    node = iota((16, LANES), 0).astype(F32)
    hits_in = jnp.where((target_own == node) & (slot_f < count_in), 1.0, 0.0)
    degree = jnp.sum(hits_in, axis=1, keepdims=True)

    og = og_ref[...]
    get_w2n.wait()
    grad_mean = dot_nt(og, w2n_ref[...]) / (1.0 + degree)
    gm_all[d] = grad_mean.astype(BF16)
    to_row(gm_all.at[d], gm_all.at[d], gm_s, gm_r)

    get_w2s.wait()
    grad_self = dot_nt(og, w2s_ref[...])
    hits_out = jnp.where((rows_own == node) & (slot_f < count_own), 1.0, 0.0)
    everyone = iota((NDP * 16, LANES), 0).astype(F32)
    table_in = jnp.where(everyone == base + rows_in, 1.0, 0.0).astype(BF16)
    table_out = jnp.where(everyone == base + target_in, 1.0, 0.0).astype(BF16)
    mix_in = dot_nt(hits_in.astype(BF16), table_in).astype(BF16)
    mix_out = dot_nt(hits_out.astype(BF16), table_out).astype(BF16)

    @pl.when(jnp.logical_not(near_column))
    def _():
        arrived(w_at(-8), wz_r.at[place(-8) % 16])
        arrived(w_relay, wr_r.at[0])
        for c in w_far_sends:
            c.start()

    arrived(relay_up, relay_r.at[0])
    for t in range(8, 0, -1):
        send(relay_up.at[t - 1], slots.at[place(-8 - t)], x_s.at[16 + t], x_r.at[place(-8 - t)], chip(t))
    arrived(relay_down, relay_r.at[1])
    for t in range(7, 0, -1):
        send(relay_down.at[7 - t], slots.at[place(8 + t)], x_s.at[24 + t], x_r.at[place(8 + t)], chip(-t))

    @pl.when(near_column)
    def _():
        for t in w_near:
            arrived(w_at(-t), wz_r.at[place(-t) % 16])
        to_row(w.at[d], w.at[d], wd_s, wd_r)

    from_row(gm_all, gm_r)
    back = dot(mix_out, gm_all[...].reshape(NDP * 16, 512))
    gh_own[...] = (grad_self + grad_mean + back).astype(BF16)
    send(gh_own, gh_relay, gh_s.at[0], gh_r.at[0], chip(8))

    arrived(xp, d2d_r.at[0])
    node_in = iota((1024, 512), 0)
    node_at = iota((1024, 512), 1)
    block_at = node_at // 16
    chip_at = lax.rem(z - 7 + NZ + block_at // 2 + 16 * lax.rem(block_at, 2), NZ)
    pick = jnp.where(node_in == 32 * chip_at + 16 * q + lax.rem(node_at, 16), 1.0, 0.0).astype(BF16)
    wide_rows = jnp.concatenate(
        [
            jnp.concatenate([buf[c, kind] for c in range(GROUPS)], axis=1)
            for buf in (xs, xp)
            for kind in (0, 1)
        ],
        axis=0,
    )
    x_cols = dot(wide_rows, pick).astype(BF16)

    @pl.when(jnp.logical_not(near_column))
    def _():
        for offset in list(range(9, 17)) + list(range(-15, -8)):
            arrived(w_at(offset), wz_r.at[place(offset) % 16])
        to_row(w.at[d], w.at[d], wd_s, wd_r)

    arrived(gh_relay, gh_r.at[0])
    send(gh_relay, gh_opp, gh_s.at[1], gh_r.at[1], chip(8))

    for offset in range(-15, 17):
        if offset:
            arrived(slots.at[place(offset)], x_r.at[place(offset)])
    turned = [
        jnp.transpose(slots[16 * half : 16 * half + 16].reshape(256, LANES).astype(F32)).astype(BF16)
        for half in (0, 1)
    ]

    def rows_of(half, kind):
        t = turned[half]
        return jnp.concatenate([t[32 * kind : 32 * kind + 32], t[64 + 32 * kind : 96 + 32 * kind]], axis=0)

    x_rows = [[rows_of(half, kind) for kind in (0, 1)] for half in (0, 1)]

    from_row(w, wd_r)
    for block in range(4):
        total = jnp.zeros((64, LANES), F32)
        for half in (0, 1):
            for kind in (0, 1):
                total += dot(x_rows[half][kind], w[half * 8 + kind * 4 + block])
        lanes = slice(LANES * block, LANES * (block + 1))
        for core in (0, 1):
            part[core, 0:16, lanes] = total[16 * core : 16 * core + 16]
            part[core, 16:32, lanes] = total[32 + 16 * core : 48 + 16 * core]

    send(part.at[1 - q], part_in, d2d_s.at[1], d2d_r.at[1], partner)
    arrived(part_in, d2d_r.at[1])
    preact = part[q] + part_in[...]
    hidden = jnp.maximum(preact[0:16], 0.0).astype(BF16)
    arrived(gh_opp, gh_r.at[1])
    gp[7, 0] = jnp.where(preact[0:16] > 0, gh_own[...].astype(F32), 0.0).astype(BF16)
    gp[7, 1] = jnp.where(preact[16:32] > 0, gh_opp[...].astype(F32), 0.0).astype(BF16)
    h_all[d] = hidden

    def pass_on(offset, targets):
        for target in targets:
            there = offset - target + 7
            send(gp.at[offset + 7], gp.at[there], gp_s.at[there], gp_r.at[there], chip(target))

    pass_on(*WINDOW_PLAN[0])
    to_row(h_all.at[d], h_all.at[d], h_s, h_r)
    for offset, targets in WINDOW_PLAN[1:]:
        arrived(gp.at[offset + 7], gp_r.at[offset + 7])
        pass_on(offset, targets)

    from_row(h_all, h_r)
    neigh_sum = dot(mix_in, h_all[...].reshape(NDP * 16, 512))
    mean_two = ((hidden.astype(F32) + neigh_sum) / (1.0 + degree)).astype(BF16)
    out_ref[...] = (dot(hidden, w2s_ref[...]) + dot(mean_two, w2n_ref[...])).astype(BF16)

    for offset in range(-7, 9):
        if offset not in (0, 5, -5):
            arrived(gp.at[offset + 7], gp_r.at[offset + 7])

    res[...] = dot(x_cols, gp[...].reshape(512, 512))
    send(res.at[32:64], res_in, d2d_s.at[2], d2d_r.at[2], partner)
    arrived(res_in, d2d_r.at[2])
    gs_ref[...] = res[0:16] + res_in[0:16]
    gn_ref[...] = res[16:32] + res_in[16:32]

    for c in sends:
        c.wait_send()

    @pl.when(near_column)
    def _():
        for c in w_near_sends:
            c.wait_send()

    @pl.when(jnp.logical_not(near_column))
    def _():
        for c in [w_up, w_down] + w_far_sends:
            c.wait_send()

    @pl.loop(1, NDP)
    def _(i):
        to = {"dp": row_peer(i)}
        copy(meta.at[d], meta.at[d], meta_s.at[i], meta_r.at[d], to).wait_send()
        copy(gm_all.at[d], gm_all.at[d], gm_s.at[i], gm_r.at[d], to).wait_send()
        copy(h_all.at[d], h_all.at[d], h_s.at[i], h_r.at[d], to).wait_send()
        copy(w.at[d], w.at[d], wd_s.at[i], wd_r.at[d], to).wait_send()


def on_device(
    features,
    neigh_lists,
    w1_self,
    w1_neigh,
    w2_self,
    w2_neigh,
    send_rows,
    send_count,
    recv_target,
    out_grad,
):
    dma = pltpu.SemaphoreType.DMA
    vmem = pl.BlockSpec(memory_space=pltpu.VMEM)
    hbm = pl.BlockSpec(memory_space=pl.ANY)
    layer_out, grad_self, grad_neigh = pl.pallas_call(
        kernel,
        out_shape=(
            jax.ShapeDtypeStruct((16, 512), BF16),
            jax.ShapeDtypeStruct((16, 512), F32),
            jax.ShapeDtypeStruct((16, 512), F32),
        ),
        in_specs=[vmem] * 4 + [hbm] * 2 + [vmem] * 4,
        out_specs=(vmem, vmem, vmem),
        scratch_shapes=[
            pltpu.VMEM((512, 512), BF16),
            pltpu.VMEM((512, 512), BF16),
            pltpu.VMEM((GROUPS, 2, 16, LANES), BF16),
            pltpu.VMEM((GROUPS, 2, 16, LANES), BF16),
            pltpu.VMEM((NZ, 16, LANES), BF16),
            pltpu.VMEM((NZ, 16, LANES), BF16),
            pltpu.VMEM((8, 16, LANES), BF16),
            pltpu.VMEM((7, 16, LANES), BF16),
            pltpu.VMEM((NDP, 256, LANES), BF16),
            pltpu.VMEM((16, LANES), BF16),
            pltpu.VMEM((16, LANES), BF16),
            pltpu.VMEM((NDP, 8, LANES), F32),
            pltpu.VMEM((NDP, 16, 512), BF16),
            pltpu.VMEM((NDP, 16, 512), BF16),
            pltpu.VMEM((16, 512), BF16),
            pltpu.VMEM((16, 512), BF16),
            pltpu.VMEM((16, 512), BF16),
            pltpu.VMEM((16, 2, 16, 512), BF16),
            pltpu.VMEM((2, 32, 512), F32),
            pltpu.VMEM((32, 512), F32),
            pltpu.VMEM((64, 512), F32),
            pltpu.VMEM((32, 512), F32),
            dma((2,)),
            dma((NZ,)),
            dma((NZ,)),
            dma((2,)),
            dma((2,)),
            dma((16,)),
            dma((16,)),
            dma((2,)),
            dma((1,)),
            dma((NDP,)),
            dma((NDP,)),
            dma((NDP,)),
            dma((NDP,)),
            dma((NDP,)),
            dma((NDP,)),
            dma((NDP,)),
            dma((NDP,)),
            dma((2,)),
            dma((2,)),
            dma((16,)),
            dma((16,)),
            dma((3,)),
            dma((3,)),
        ],
        compiler_params=pltpu.CompilerParams(
            collective_id=0, has_side_effects=True, vmem_limit_bytes=40 * 1024 * 1024
        ),
    )(
        features[0],
        jnp.transpose(neigh_lists, (1, 0, 2)),
        w1_self,
        w1_neigh,
        w2_self,
        w2_neigh,
        jnp.transpose(send_rows[0, 0]),
        send_count[0],
        jnp.transpose(recv_target[0, 0]),
        out_grad[0, 0],
    )
    return layer_out[None, None], grad_self[None], grad_neigh[None]


def solution(mesh):
    in_specs = (
        P("dp", "feat", None),
        P("dp", None, None),
        P("feat", None),
        P("feat", None),
        P(),
        P(),
        P("dp", "feat", None, None),
        P("dp", "feat", None),
        P("dp", "feat", None, None),
        P("dp", "feat", None, None),
    )
    out_specs = (P("dp", "feat", None, None), P("dp", "feat", None), P("dp", "feat", None))
    return jax.shard_map(
        on_device, mesh=mesh, in_specs=in_specs, out_specs=out_specs, check_vma=False
    )
```

time: 94 us -> 89.8 us (0.955)
  the two profiles are of different devices: /device:TPU:1 before, /device:TPU:33 now
where the time goes in v2:
time: 89.8 us; the launch traced here: 89.2 us
  Pallas kernels  80.2 us (89%)
  local copies, waits for them, and re-layouts  8.37 us (9%)
    pallas_call x1, Pallas kernels, on_device(): pl.pallas_call(kernel, out_shape=(jax.ShapeDtypeStruct((16, 512), BF16),...  80.2 us
    unnamed x23, local copies, waits for them, and re-layouts  8.37 us

profile of v2, /device:TPU:33, one launch (start us, length us, event | category | flops | bytes accessed | tf_op | source)
XLA Modules:
  0.0 89.2 jit_solution(4063361605368859584)
XLA Ops:
  0.6 0.0 copy-start.8
  0.6 0.0 copy-start.7
  0.7 0.0 copy-start.9
  0.7 0.7 copy-done.8
  1.3 0.0 copy-done.7
  1.3 0.0 copy-done.9
  1.3 0.0 copy-start
  1.3 1.0 %copy-done = bf16[512,512]{1,0:T(8,128)(2,1)S(1)} copy-done((bf16[512,512]{1,0:T(8,128)(2,1)S(1)}, bf16[512,512]{1,0:T(8,128)(2,1)}, u32[]{:S(2)}) %copy-start) | copy-done | bytes 524312
  2.4 0.0 copy-start.1
  2.4 1.0 %copy-done.1 = bf16[512,512]{1,0:T(8,128)(2,1)S(1)} copy-done((bf16[512,512]{1,0:T(8,128)(2,1)S(1)}, bf16[512,512]{1,0:T(8,128)(2,1)}, u32[]{:S(2)}) %copy-start.1) | copy-done | bytes 524312
  3.4 0.0 copy-start.2
  3.4 0.8 copy-done.2
  4.3 0.0 copy-start.3
  4.3 0.8 copy-done.3
  5.0 0.0 copy-start.4
  5.0 0.7 copy-done.4
  5.8 0.0 copy-start.5
  5.8 0.7 copy-done.5
  6.5 0.0 copy-start.6
  6.5 0.7 copy-done.6
  7.2 80.2 %shard_map.121 = (bf16[16,512]{1,0:T(8,128)(2,1)S(1)}, f32[16,512]{1,0:T(8,128)S(1)}, f32[16,512]{1,0:T(8,128)S(1)}) custom-call(bf16[16,2048]{1,0:T(8,128)(2,1)S(1)} %bitcast.13, s32[10,1,1024]{2,1,0:T(1,128)S(1)} %bitcast.14, bf16[16,512]{1,0:T(8,128)(2,1)S(1)} %copy-done.4, bf16[16,512]{1,0:T(8,128)(2,1)S(1)} %copy-done.5, bf16[512,512]{1,0:T(8,128)(2,1)S(1)} %copy-done, ...), custom_call_target="tpu_custom_call" | custom-call | tf_op jit(solution)/shard_map/pallas_call | solution.py:435
  87.4 0.6 copy.16
  88.0 0.6 copy.17
  88.6 0.6 copy.18
Async XLA Ops:
  0.6 0.7 copy-start.8
  0.6 0.7 copy-start.7
  0.7 0.7 copy-start.9
  1.3 1.0 %copy-start = (bf16[512,512]{1,0:T(8,128)(2,1)S(1)}, bf16[512,512]{1,0:T(8,128)(2,1)}, u32[]{:S(2)}) copy-start(bf16[512,512]{1,0:T(8,128)(2,1)} %w2s_hbm.1) | copy-start | bytes 1572868
  2.4 1.0 %copy-start.1 = (bf16[512,512]{1,0:T(8,128)(2,1)S(1)}, bf16[512,512]{1,0:T(8,128)(2,1)}, u32[]{:S(2)}) copy-start(bf16[512,512]{1,0:T(8,128)(2,1)} %w2n_hbm.1) | copy-start | bytes 1572868
  3.4 0.8 copy-start.2
  4.3 0.8 copy-start.3
  5.0 0.7 copy-start.4
  5.8 0.7 copy-start.5
  6.5 0.7 copy-start.6

commit v3 on v2

--- a/solution.py
+++ b/solution.py
@@ -40,12 +40,25 @@
 
 
 def kernel(
+    feat_in,
+    lists_in,
+    w1s_in,
+    w1n_in,
+    w2s_in,
+    w2n_in,
+    rows_in_hbm,
+    count_in_hbm,
+    target_in_hbm,
+    og_in,
+    out_hbm,
+    gs_hbm,
+    gn_hbm,
     feat_ref,
     lists_ref,
     w1s_ref,
     w1n_ref,
-    w2s_hbm,
-    w2n_hbm,
+    w2s_ref,
+    w2n_ref,
     rows_ref,
     count_ref,
     target_ref,
@@ -53,8 +66,6 @@
     out_ref,
     gs_ref,
     gn_ref,
-    w2s_ref,
-    w2n_ref,
     xs,
     xp,
     tiles,
@@ -137,6 +148,22 @@
             e = row_peer(i)
             arrived(buf.at[e], recv_sem.at[e])
 
+    pairs = (
+        (feat_in, feat_ref),
+        (lists_in, lists_ref),
+        (rows_in_hbm, rows_ref),
+        (count_in_hbm, count_ref),
+        (target_in_hbm, target_ref),
+        (w1s_in, w1s_ref),
+        (w1n_in, w1n_ref),
+        (og_in, og_ref),
+        (w2n_in, w2n_ref),
+        (w2s_in, w2s_ref),
+    )
+    loads = [pltpu.make_async_copy(src, dst, local_s.at[n]) for n, (src, dst) in enumerate(pairs)]
+    for c in loads[:2]:
+        c.start()
+
     barrier = pltpu.get_barrier_semaphore()
 
     def signal(device):
@@ -151,10 +178,10 @@
     def _(i):
         signal({"dp": row_peer(i)})
 
-    get_w2s = pltpu.make_async_copy(w2s_hbm, w2s_ref, local_s.at[0])
-    get_w2n = pltpu.make_async_copy(w2n_hbm, w2n_ref, local_s.at[1])
-    get_w2s.start()
-    get_w2n.start()
+    for c in loads[2:]:
+        c.start()
+    for c in loads[:2]:
+        c.wait()
 
     chunks = [feat_ref[:, LANES * i : LANES * (i + 1)].astype(F32) for i in range(16)]
 
@@ -197,6 +224,9 @@
     spread = peer_rows.astype(F32).astype(BF16)
     own_slot = iota((8, LANES), 0) == lax.rem(iota((8, LANES), 1), 8)
 
+    for c in loads[2:7]:
+        c.wait()
+
     def flat(ref):
         wide = dot(ref[...].astype(F32).astype(BF16), spread)
         return jnp.sum(jnp.where(own_slot, wide, 0.0), axis=0, keepdims=True)
@@ -270,13 +300,14 @@
     hits_in = jnp.where((target_own == node) & (slot_f < count_in), 1.0, 0.0)
     degree = jnp.sum(hits_in, axis=1, keepdims=True)
 
+    loads[7].wait()
+    loads[8].wait()
     og = og_ref[...]
-    get_w2n.wait()
     grad_mean = dot_nt(og, w2n_ref[...]) / (1.0 + degree)
     gm_all[d] = grad_mean.astype(BF16)
     to_row(gm_all.at[d], gm_all.at[d], gm_s, gm_r)
 
-    get_w2s.wait()
+    loads[9].wait()
     grad_self = dot_nt(og, w2s_ref[...])
     hits_out = jnp.where((rows_own == node) & (slot_f < count_own), 1.0, 0.0)
     everyone = iota((NDP * 16, LANES), 0).astype(F32)
@@ -381,9 +412,14 @@
         pass_on(offset, targets)
 
     from_row(h_all, h_r)
+    stores = [
+        pltpu.make_async_copy(src, dst, local_s.at[10 + n])
+        for n, (src, dst) in enumerate(((out_ref, out_hbm), (gs_ref, gs_hbm), (gn_ref, gn_hbm)))
+    ]
     neigh_sum = dot(mix_in, h_all[...].reshape(NDP * 16, 512))
     mean_two = ((hidden.astype(F32) + neigh_sum) / (1.0 + degree)).astype(BF16)
     out_ref[...] = (dot(hidden, w2s_ref[...]) + dot(mean_two, w2n_ref[...])).astype(BF16)
+    stores[0].start()
 
     for offset in range(-7, 9):
         if offset not in (0, 5, -5):
@@ -394,6 +430,9 @@
     arrived(res_in, d2d_r.at[2])
     gs_ref[...] = res[0:16] + res_in[0:16]
     gn_ref[...] = res[16:32] + res_in[16:32]
+
+    stores[1].start()
+    stores[2].start()
 
     for c in sends:
         c.wait_send()
@@ -415,6 +454,9 @@
         copy(gm_all.at[d], gm_all.at[d], gm_s.at[i], gm_r.at[d], to).wait_send()
         copy(h_all.at[d], h_all.at[d], h_s.at[i], h_r.at[d], to).wait_send()
         copy(w.at[d], w.at[d], wd_s.at[i], wd_r.at[d], to).wait_send()
+
+    for c in stores:
+        c.wait()
 
 
 def on_device(
@@ -430,7 +472,6 @@
     out_grad,
 ):
     dma = pltpu.SemaphoreType.DMA
-    vmem = pl.BlockSpec(memory_space=pltpu.VMEM)
     hbm = pl.BlockSpec(memory_space=pl.ANY)
     layer_out, grad_self, grad_neigh = pl.pallas_call(
         kernel,
@@ -439,11 +480,22 @@
             jax.ShapeDtypeStruct((16, 512), F32),
             jax.ShapeDtypeStruct((16, 512), F32),
         ),
-        in_specs=[vmem] * 4 + [hbm] * 2 + [vmem] * 4,
-        out_specs=(vmem, vmem, vmem),
+        in_specs=[hbm] * 10,
+        out_specs=(hbm, hbm, hbm),
         scratch_shapes=[
+            pltpu.VMEM((16, 2048), BF16),
+            pltpu.VMEM((K1, 1, 1024), jnp.int32),
+            pltpu.VMEM((16, 512), BF16),
+            pltpu.VMEM((16, 512), BF16),
             pltpu.VMEM((512, 512), BF16),
             pltpu.VMEM((512, 512), BF16),
+            pltpu.VMEM((8, 16), jnp.int32),
+            pltpu.VMEM((1, 16), jnp.int32),
+            pltpu.VMEM((8, 16), jnp.int32),
+            pltpu.VMEM((16, 512), BF16),
+            pltpu.VMEM((16, 512), BF16),
+            pltpu.VMEM((16, 512), F32),
+            pltpu.VMEM((16, 512), F32),
             pltpu.VMEM((GROUPS, 2, 16, LANES), BF16),
             pltpu.VMEM((GROUPS, 2, 16, LANES), BF16),
             pltpu.VMEM((NZ, 16, LANES), BF16),
@@ -464,7 +516,7 @@
             pltpu.VMEM((32, 512), F32),
             pltpu.VMEM((64, 512), F32),
             pltpu.VMEM((32, 512), F32),
-            dma((2,)),
+            dma((13,)),
             dma((NZ,)),
             dma((NZ,)),
             dma((2,)),
@@ -489,7 +541,7 @@
             dma((3,)),
         ],
         compiler_params=pltpu.CompilerParams(
-            collective_id=0, has_side_effects=True, vmem_limit_bytes=40 * 1024 * 1024
+            collective_id=0, has_side_effects=True, vmem_limit_bytes=64 * 1024 * 1024
         ),
     )(
         features[0],

time: 89.8 us -> 84.3 us (0.939)
  local copies, waits for them, and re-layouts: 8.37 us -> 2.72 us
    unnamed x23 -> x7, local copies, waits for them, and re-layouts: 8.37 us -> 2.72 us
where the time goes in v3:
time: 84.3 us; the launch traced here: 84 us
  Pallas kernels  80.6 us (96%)
  local copies, waits for them, and re-layouts  2.72 us (3%)
    pallas_call x1, Pallas kernels, on_device(): pl.pallas_call(kernel, out_shape=(jax.ShapeDtypeStruct((16, 512), BF16),...  80.6 us
    unnamed x7, local copies, waits for them, and re-layouts  2.72 us

profile of v3, /device:TPU:33, one launch (start us, length us, event | category | flops | bytes accessed | tf_op | source)
XLA Modules:
  0.0 84.0 jit_solution(5481318922510870674)
XLA Ops:
  0.6 80.6 %shard_map.121 = (bf16[16,512]{1,0:T(8,128)(2,1)}, f32[16,512]{1,0:T(8,128)}, f32[16,512]{1,0:T(8,128)}) custom-call(bf16[16,2048]{1,0:T(8,128)(2,1)} %bitcast.13, s32[10,1,1024]{2,1,0:T(1,128)} %bitcast.14, bf16[16,512]{1,0:T(8,128)(2,1)} %w1s_in.1, bf16[16,512]{1,0:T(8,128)(2,1)} %w1n_in.1, bf16[512,512]{1,0:T(8,128)(2,1)} %w2s_in.1, ...), custom_call_target="tpu_custom_call" | custom-call | tf_op jit(solution)/shard_map/pallas_call | solution.py:476
  81.3 0.0 copy-start.1
  81.3 1.3 %copy.16 = bf16[1,1,16,512]{3,2,1,0:T(8,128)(2,1)} copy(bf16[1,1,16,512]{3,2,1,0:T(8,128)(2,1)} %bitcast.18) | data formatting | bytes 32768
  82.6 0.0 copy-done.1
  82.6 0.0 copy-start
  82.6 0.6 copy.17
  83.2 0.2 copy-done
  83.4 0.6 copy.18
Async XLA Ops:
  81.3 1.3 %copy-start.1 = (f32[16,512]{1,0:T(8,128)S(1)}, f32[16,512]{1,0:T(8,128)}, u32[]{:S(2)}) copy-start(f32[16,512]{1,0:T(8,128)} %get-tuple-element.7) | copy-start | bytes 98308
  82.6 0.8 copy-start

commit v4 on v3

--- a/solution.py
+++ b/solution.py
@@ -1,3 +1,5 @@
+import functools
+
 import jax
 import jax.numpy as jnp
 from jax import lax
@@ -15,7 +17,7 @@
 BF16 = jnp.bfloat16
 
 WINDOW_PLAN = (
-    (0, (-8, 5, -5, 2, -2, 1, -1)),
+    (0, (5, -5, -8, 2, -2, 1, -1)),
     (5, (2, -2, 1, -1)),
     (-5, (2, -2, 1, -1)),
 )
@@ -24,7 +26,14 @@
 def place(offset):
     if offset <= -16:
         offset += NZ
-    return offset + 7 if offset >= -7 else 16 - offset
+    if -7 <= offset <= 8:
+        at = (offset + 7) // 2
+    else:
+        at = 8 + (offset - 9) // 2 if offset > 0 else 12 + (-offset - 8) // 2
+    return offset % 2 * 16 + at
+
+
+assert sorted(place(o) for o in range(-15, 17)) == list(range(NZ))
 
 
 def iota(shape, axis):
@@ -79,7 +88,6 @@
     gm_all,
     h_all,
     gh_own,
-    gh_relay,
     gh_opp,
     gp,
     part,
@@ -93,7 +101,6 @@
     relay_r,
     wz_s,
     wz_r,
-    wr_s,
     wr_r,
     wd_s,
     wd_r,
@@ -105,6 +112,7 @@
     h_r,
     gh_s,
     gh_r,
+    hello,
     gp_s,
     gp_r,
     d2d_s,
@@ -238,11 +246,11 @@
 
     piece = lax.rem(d, 8)
     w_lanes = pl.ds(pl.multiple_of(lax.rem(d, 4) * LANES, LANES), LANES)
-    near_column = d < 8
+    parity = d // 8
     own_tile = jnp.where(piece < 4, w1s_ref[:, w_lanes].astype(F32), w1n_ref[:, w_lanes].astype(F32)).astype(BF16)
     w_own[...] = own_tile
 
-    @pl.when(near_column)
+    @pl.when(parity == 0)
     def _():
         w[d, pl.ds(16 * place(0), 16), :] = own_tile
 
@@ -254,34 +262,73 @@
     send(tiles.at[pl.ds(9, 8)], relay_up, relay_s.at[0], relay_r.at[0], chip(8))
     send(tiles.at[pl.ds(17, 7)], relay_down, relay_s.at[1], relay_r.at[1], chip(-8))
 
-    w_near = [t for k in range(8, 0, -1) for t in (-k, k) if t != 8]
-    w_near_sends = [
-        copy(w_own, w_at(-t), wz_s.at[n], wz_r.at[place(-t) % 16], chip(t)) for n, t in enumerate(w_near)
-    ]
-    w_up = copy(w_own, w_at(-8), wr_s.at[0], wz_r.at[place(-8) % 16], chip(8))
-    w_down = copy(w_own, w_relay, wr_s.at[1], wr_r.at[0], chip(-8))
-    w_far_sends = [
-        copy(w_at(-8), w_at(-8 - t), wz_s.at[t - 1], wz_r.at[place(-8 - t) % 16], chip(t)) for t in range(8, 0, -1)
-    ] + [
-        copy(w_relay, w_at(8 + t), wz_s.at[7 + t], wz_r.at[place(8 + t) % 16], chip(-t)) for t in range(7, 0, -1)
-    ]
-
-    @pl.when(jnp.logical_not(near_column))
-    def _():
-        w_up.start()
-        w_down.start()
+    w_direct, w_passed, w_near, w_far = [], [], [], []
+    for p in (0, 1):
+        up, down = (w_at(-8), w_at(8)) if p == 0 else (w_relay.at[0], w_relay.at[1])
+        up_sem, down_sem = (
+            (wz_r.at[place(-8) % 16], wz_r.at[place(8) % 16]) if p == 0 else (wr_r.at[0], wr_r.at[1])
+        )
+        near = [t for k in range(7, 0, -1) for t in (k, -k) if k % 2 == p]
+        direct = [(8, up, up_sem), (-8, down, down_sem)]
+        direct += [(t, w_at(-t), wz_r.at[place(-t) % 16]) for t in near]
+        w_direct.append([copy(w_own, dst, wz_s.at[n], sem, chip(t)) for n, (t, dst, sem) in enumerate(direct)])
+        passed = [(up, -8 - t, t) for t in range(8, 0, -1) if t % 2 == p]
+        passed += [(down, 8 + t, -t) for t in range(7, 0, -1) if t % 2 == p]
+        w_passed.append(
+            [
+                copy(src, w_at(offset), wz_s.at[10 + n], wz_r.at[place(offset) % 16], chip(t))
+                for n, (src, offset, t) in enumerate(passed)
+            ]
+        )
+        w_near.append(near)
+        w_far.append([offset + (NZ if offset == -16 else 0) for _, offset, _ in passed])
+
+    def by_parity(body):
+        for p in (0, 1):
+            pl.when(parity == p)(functools.partial(body, p))
+
+    def start_weights(p):
+        for c in w_direct[p]:
+            c.start()
+
+    def pass_weights(p):
+        if p == 0:
+            arrived(w_at(-8), wz_r.at[place(-8) % 16])
+            arrived(w_at(8), wz_r.at[place(8) % 16])
+        else:
+            arrived(w_relay.at[0], wr_r.at[0])
+            arrived(w_relay.at[1], wr_r.at[1])
+        for c in w_passed[p]:
+            c.start()
+        for t in w_near[p]:
+            arrived(w_at(-t), wz_r.at[place(-t) % 16])
+
+    def far_weights(p):
+        for offset in w_far[p]:
+            arrived(w_at(offset), wz_r.at[place(offset) % 16])
+
+    def sent_weights(p):
+        for c in w_direct[p] + w_passed[p]:
+            c.wait_send()
+
+    by_parity(start_weights)
 
     for k in range(8, 0, -1):
         for t in (k, -k):
             send(tiles.at[t % NZ], slots.at[place(-t)], x_s.at[t + 8], x_r.at[place(-t)], chip(t))
 
-    @pl.when(near_column)
-    def _():
-        for c in w_near_sends:
-            c.start()
-
     to_row(meta.at[d], meta.at[d], meta_s, meta_r)
+
+    loads[7].wait()
+    loads[8].wait()
+    og = og_ref[...]
+    raw_mean = dot_nt(og, w2n_ref[...])
+    gm_all[d] = raw_mean.astype(BF16)
+    to_row(gm_all.at[d], gm_all.at[d], gm_s, gm_r)
+    pl.semaphore_signal(hello, inc=1, device_id=chip(8), device_id_type=MESH)
     send(xs, xp, d2d_s.at[0], d2d_r.at[0], partner)
+    loads[9].wait()
+    grad_self = dot_nt(og, w2s_ref[...])
 
     from_row(meta, meta_r)
     mine = iota((NDP, LANES), 1) // 8 == d
@@ -300,15 +347,6 @@
     hits_in = jnp.where((target_own == node) & (slot_f < count_in), 1.0, 0.0)
     degree = jnp.sum(hits_in, axis=1, keepdims=True)
 
-    loads[7].wait()
-    loads[8].wait()
-    og = og_ref[...]
-    grad_mean = dot_nt(og, w2n_ref[...]) / (1.0 + degree)
-    gm_all[d] = grad_mean.astype(BF16)
-    to_row(gm_all.at[d], gm_all.at[d], gm_s, gm_r)
-
-    loads[9].wait()
-    grad_self = dot_nt(og, w2s_ref[...])
     hits_out = jnp.where((rows_own == node) & (slot_f < count_own), 1.0, 0.0)
     everyone = iota((NDP * 16, LANES), 0).astype(F32)
     table_in = jnp.where(everyone == base + rows_in, 1.0, 0.0).astype(BF16)
@@ -316,12 +354,20 @@
     mix_in = dot_nt(hits_in.astype(BF16), table_in).astype(BF16)
     mix_out = dot_nt(hits_out.astype(BF16), table_out).astype(BF16)
 
-    @pl.when(jnp.logical_not(near_column))
-    def _():
-        arrived(w_at(-8), wz_r.at[place(-8) % 16])
-        arrived(w_relay, wr_r.at[0])
-        for c in w_far_sends:
-            c.start()
+    first_lane = (iota((NDP, LANES), 1) == 8 * iota((NDP, LANES), 0)).astype(F32).astype(BF16)
+    count_to = dot_nt(first_lane, meta[:, 2, :].astype(BF16)).astype(BF16)
+    live = lax.rem(iota((NDP, LANES), 1), 8).astype(F32) < dot(count_to, spread)
+    aims = jnp.where(live, meta[:, 1, :], 31.0).astype(BF16)
+    repeat = (iota((NDP * 16, NDP), 0) // 16 == iota((NDP * 16, NDP), 1)).astype(F32).astype(BF16)
+    hits = dot(repeat, aims) == lax.rem(iota((NDP * 16, LANES), 0), 16).astype(F32)
+    degrees = jnp.sum(jnp.where(hits, 1.0, 0.0), axis=1, keepdims=True)
+
+    from_row(gm_all, gm_r)
+    returned = gm_all[...].reshape(NDP * 16, 512).astype(F32) / (1.0 + degrees)
+    back = jnp.dot(mix_out.astype(F32), returned, precision=lax.Precision.HIGHEST, preferred_element_type=F32)
+    gh_own[...] = (grad_self + raw_mean / (1.0 + degree) + back).astype(BF16)
+    pl.semaphore_wait(hello, 1)
+    send(gh_own, gh_opp, gh_s.at[0], gh_r.at[0], chip(16))
 
     arrived(relay_up, relay_r.at[0])
     for t in range(8, 0, -1):
@@ -330,16 +376,10 @@
     for t in range(7, 0, -1):
         send(relay_down.at[7 - t], slots.at[place(8 + t)], x_s.at[24 + t], x_r.at[place(8 + t)], chip(-t))
 
-    @pl.when(near_column)
-    def _():
-        for t in w_near:
-            arrived(w_at(-t), wz_r.at[place(-t) % 16])
-        to_row(w.at[d], w.at[d], wd_s, wd_r)
-
-    from_row(gm_all, gm_r)
-    back = dot(mix_out, gm_all[...].reshape(NDP * 16, 512))
-    gh_own[...] = (grad_self + grad_mean + back).astype(BF16)
-    send(gh_own, gh_relay, gh_s.at[0], gh_r.at[0], chip(8))
+    by_parity(pass_weights)
+    early = pl.ds(0, 128)
+    late = pl.ds(128, 128)
+    to_row(w.at[d, early], w.at[d, early], wd_s.at[0], wd_r.at[0])
 
     arrived(xp, d2d_r.at[0])
     node_in = iota((1024, 512), 0)
@@ -357,14 +397,8 @@
     )
     x_cols = dot(wide_rows, pick).astype(BF16)
 
-    @pl.when(jnp.logical_not(near_column))
-    def _():
-        for offset in list(range(9, 17)) + list(range(-15, -8)):
-            arrived(w_at(offset), wz_r.at[place(offset) % 16])
-        to_row(w.at[d], w.at[d], wd_s, wd_r)
-
-    arrived(gh_relay, gh_r.at[0])
-    send(gh_relay, gh_opp, gh_s.at[1], gh_r.at[1], chip(8))
+    by_parity(far_weights)
+    to_row(w.at[d, late], w.at[d, late], wd_s.at[1], wd_r.at[1])
 
     for offset in range(-15, 17):
         if offset:
@@ -380,7 +414,12 @@
 
     x_rows = [[rows_of(half, kind) for kind in (0, 1)] for half in (0, 1)]
 
-    from_row(w, wd_r)
+    @pl.loop(1, NDP)
+    def _(i):
+        e = row_peer(i)
+        arrived(w.at[e, early], wd_r.at[0, e])
+        arrived(w.at[e, late], wd_r.at[1, e])
+
     for block in range(4):
         total = jnp.zeros((64, LANES), F32)
         for half in (0, 1):
@@ -395,7 +434,7 @@
     arrived(part_in, d2d_r.at[1])
     preact = part[q] + part_in[...]
     hidden = jnp.maximum(preact[0:16], 0.0).astype(BF16)
-    arrived(gh_opp, gh_r.at[1])
+    arrived(gh_opp, gh_r.at[0])
     gp[7, 0] = jnp.where(preact[0:16] > 0, gh_own[...].astype(F32), 0.0).astype(BF16)
     gp[7, 1] = jnp.where(preact[16:32] > 0, gh_opp[...].astype(F32), 0.0).astype(BF16)
     h_all[d] = hidden
@@ -437,15 +476,7 @@
     for c in sends:
         c.wait_send()
 
-    @pl.when(near_column)
-    def _():
-        for c in w_near_sends:
-            c.wait_send()
-
-    @pl.when(jnp.logical_not(near_column))
-    def _():
-        for c in [w_up, w_down] + w_far_sends:
-            c.wait_send()
+    by_parity(sent_weights)
 
     @pl.loop(1, NDP)
     def _(i):
@@ -453,7 +484,8 @@
         copy(meta.at[d], meta.at[d], meta_s.at[i], meta_r.at[d], to).wait_send()
         copy(gm_all.at[d], gm_all.at[d], gm_s.at[i], gm_r.at[d], to).wait_send()
         copy(h_all.at[d], h_all.at[d], h_s.at[i], h_r.at[d], to).wait_send()
-        copy(w.at[d], w.at[d], wd_s.at[i], wd_r.at[d], to).wait_send()
+        copy(w.at[d, early], w.at[d, early], wd_s.at[0, i], wd_r.at[0, d], to).wait_send()
+        copy(w.at[d, late], w.at[d, late], wd_s.at[1, i], wd_r.at[1, d], to).wait_send()
 
     for c in stores:
         c.wait()
@@ -504,11 +536,10 @@
             pltpu.VMEM((7, 16, LANES), BF16),
             pltpu.VMEM((NDP, 256, LANES), BF16),
             pltpu.VMEM((16, LANES), BF16),
-            pltpu.VMEM((16, LANES), BF16),
+            pltpu.VMEM((2, 16, LANES), BF16),
             pltpu.VMEM((NDP, 8, LANES), F32),
             pltpu.VMEM((NDP, 16, 512), BF16),
             pltpu.VMEM((NDP, 16, 512), BF16),
-            pltpu.VMEM((16, 512), BF16),
             pltpu.VMEM((16, 512), BF16),
             pltpu.VMEM((16, 512), BF16),
             pltpu.VMEM((16, 2, 16, 512), BF16),
@@ -521,20 +552,20 @@
             dma((NZ,)),
             dma((2,)),
             dma((2,)),
-            dma((16,)),
+            dma((18,)),
             dma((16,)),
             dma((2,)),
-            dma((1,)),
+            dma((2, NDP)),
+            dma((2, NDP)),
             dma((NDP,)),
             dma((NDP,)),
             dma((NDP,)),
             dma((NDP,)),
             dma((NDP,)),
             dma((NDP,)),
-            dma((NDP,)),
-            dma((NDP,)),
-            dma((2,)),
-            dma((2,)),
+            dma((1,)),
+            dma((1,)),
+            pltpu.SemaphoreType.REGULAR,
             dma((16,)),
             dma((16,)),
             dma((3,)),

time: 84.3 us -> 81.6 us (0.968)
  the two profiles are of different devices: /device:TPU:33 before, /device:TPU:1 now
where the time goes in v4:
time: 81.6 us; the launch traced here: 81.3 us
  Pallas kernels  77.9 us (95%)
  local copies, waits for them, and re-layouts  2.72 us (3%)
    pallas_call x1, Pallas kernels, on_device(): pl.pallas_call(kernel, out_shape=(jax.ShapeDtypeStruct((16, 512), BF16),...  77.9 us
    unnamed x7, local copies, waits for them, and re-layouts  2.72 us

profile of v4, /device:TPU:1, one launch (start us, length us, event | category | flops | bytes accessed | tf_op | source)
XLA Modules:
  0.0 81.3 jit_solution(12801272017105045201)
XLA Ops:
  0.6 77.9 %shard_map.121 = (bf16[16,512]{1,0:T(8,128)(2,1)}, f32[16,512]{1,0:T(8,128)}, f32[16,512]{1,0:T(8,128)}) custom-call(bf16[16,2048]{1,0:T(8,128)(2,1)} %bitcast.13, s32[10,1,1024]{2,1,0:T(1,128)} %bitcast.14, bf16[16,512]{1,0:T(8,128)(2,1)} %w1s_in.1, bf16[16,512]{1,0:T(8,128)(2,1)} %w1n_in.1, bf16[512,512]{1,0:T(8,128)(2,1)} %w2s_in.1, ...), custom_call_target="tpu_custom_call" | custom-call | tf_op jit(solution)/shard_map/pallas_call | solution.py:508
  78.6 0.0 copy-start.1
  78.6 1.3 %copy.16 = bf16[1,1,16,512]{3,2,1,0:T(8,128)(2,1)} copy(bf16[1,1,16,512]{3,2,1,0:T(8,128)(2,1)} %bitcast.18) | data formatting | bytes 32768
  79.9 0.0 copy-done.1
  79.9 0.0 copy-start
  79.9 0.6 copy.17
  80.5 0.2 copy-done
  80.7 0.6 copy.18
Async XLA Ops:
  78.6 1.3 %copy-start.1 = (f32[16,512]{1,0:T(8,128)S(1)}, f32[16,512]{1,0:T(8,128)}, u32[]{:S(2)}) copy-start(f32[16,512]{1,0:T(8,128)} %get-tuple-element.7) | copy-start | bytes 98308
  79.9 0.8 copy-start

commit v5 on v4

--- a/solution.py
+++ b/solution.py
@@ -29,7 +29,8 @@
     if -7 <= offset <= 8:
         at = (offset + 7) // 2
     else:
-        at = 8 + (offset - 9) // 2 if offset > 0 else 12 + (-offset - 8) // 2
+        step = (offset - 9) // 2 if offset > 0 else (-offset - 8) // 2
+        at = 8 + 4 * (step // 2) + step % 2 + (0 if offset > 0 else 2)
     return offset % 2 * 16 + at
 
 
@@ -303,9 +304,10 @@
         for t in w_near[p]:
             arrived(w_at(-t), wz_r.at[place(-t) % 16])
 
-    def far_weights(p):
+    def far_weights(p, first):
         for offset in w_far[p]:
-            arrived(w_at(offset), wz_r.at[place(offset) % 16])
+            if (place(offset) % 16 < 12) == first:
+                arrived(w_at(offset), wz_r.at[place(offset) % 16])
 
     def sent_weights(p):
         for c in w_direct[p] + w_passed[p]:
@@ -377,9 +379,18 @@
         send(relay_down.at[7 - t], slots.at[place(8 + t)], x_s.at[24 + t], x_r.at[place(8 + t)], chip(-t))
 
     by_parity(pass_weights)
-    early = pl.ds(0, 128)
-    late = pl.ds(128, 128)
-    to_row(w.at[d, early], w.at[d, early], wd_s.at[0], wd_r.at[0])
+    spans = (pl.ds(0, 128), pl.ds(128, 64), pl.ds(192, 64))
+
+    def weights_to_row(n):
+        to_row(w.at[d, spans[n]], w.at[d, spans[n]], wd_s.at[n], wd_r.at[n])
+
+    def weights_from_row(n):
+        @pl.loop(1, NDP)
+        def _(i):
+            e = row_peer(i)
+            arrived(w.at[e, spans[n]], wd_r.at[n, e])
+
+    weights_to_row(0)
 
     arrived(xp, d2d_r.at[0])
     node_in = iota((1024, 512), 0)
@@ -397,8 +408,10 @@
     )
     x_cols = dot(wide_rows, pick).astype(BF16)
 
-    by_parity(far_weights)
-    to_row(w.at[d, late], w.at[d, late], wd_s.at[1], wd_r.at[1])
+    by_parity(functools.partial(far_weights, first=True))
+    weights_to_row(1)
+    by_parity(functools.partial(far_weights, first=False))
+    weights_to_row(2)
 
     for offset in range(-15, 17):
         if offset:
@@ -414,17 +427,19 @@
 
     x_rows = [[rows_of(half, kind) for kind in (0, 1)] for half in (0, 1)]
 
-    @pl.loop(1, NDP)
-    def _(i):
-        e = row_peer(i)
-        arrived(w.at[e, early], wd_r.at[0, e])
-        arrived(w.at[e, late], wd_r.at[1, e])
-
-    for block in range(4):
+    def products(block, k):
         total = jnp.zeros((64, LANES), F32)
         for half in (0, 1):
             for kind in (0, 1):
-                total += dot(x_rows[half][kind], w[half * 8 + kind * 4 + block])
+                total += dot(x_rows[half][kind][:, k], w[half * 8 + kind * 4 + block, k])
+        return total
+
+    weights_from_row(0)
+    first_sums = [products(block, slice(0, 128)) for block in range(4)]
+    weights_from_row(1)
+    weights_from_row(2)
+    for block in range(4):
+        total = first_sums[block] + products(block, slice(128, 256))
         lanes = slice(LANES * block, LANES * (block + 1))
         for core in (0, 1):
             part[core, 0:16, lanes] = total[16 * core : 16 * core + 16]
@@ -461,7 +476,7 @@
     stores[0].start()
 
     for offset in range(-7, 9):
-        if offset not in (0, 5, -5):
+        if offset not in [o for o, _ in WINDOW_PLAN]:
             arrived(gp.at[offset + 7], gp_r.at[offset + 7])
 
     res[...] = dot(x_cols, gp[...].reshape(512, 512))
@@ -484,8 +499,8 @@
         copy(meta.at[d], meta.at[d], meta_s.at[i], meta_r.at[d], to).wait_send()
         copy(gm_all.at[d], gm_all.at[d], gm_s.at[i], gm_r.at[d], to).wait_send()
         copy(h_all.at[d], h_all.at[d], h_s.at[i], h_r.at[d], to).wait_send()
-        copy(w.at[d, early], w.at[d, early], wd_s.at[0, i], wd_r.at[0, d], to).wait_send()
-        copy(w.at[d, late], w.at[d, late], wd_s.at[1, i], wd_r.at[1, d], to).wait_send()
+        for n in range(3):
+            copy(w.at[d, spans[n]], w.at[d, spans[n]], wd_s.at[n, i], wd_r.at[n, d], to).wait_send()
 
     for c in stores:
         c.wait()
@@ -555,8 +570,8 @@
             dma((18,)),
             dma((16,)),
             dma((2,)),
-            dma((2, NDP)),
-            dma((2, NDP)),
+            dma((3, NDP)),
+            dma((3, NDP)),
             dma((NDP,)),
             dma((NDP,)),
             dma((NDP,)),

time: 81.6 us -> 81.2 us (level)
  no operation moved by 1% of the time
where the time goes in v5:
time: 81.2 us; the launch traced here: 80.9 us
  Pallas kernels  77.5 us (95%)
  local copies, waits for them, and re-layouts  2.72 us (3%)
    pallas_call x1, Pallas kernels, on_device(): pl.pallas_call(kernel, out_shape=(jax.ShapeDtypeStruct((16, 512), BF16),...  77.5 us
    unnamed x7, local copies, waits for them, and re-layouts  2.72 us

profile of v5, /device:TPU:1, one launch (start us, length us, event | category | flops | bytes accessed | tf_op | source)
XLA Modules:
  0.0 80.9 jit_solution(6112199716911776104)
XLA Ops:
  0.6 77.5 %shard_map.121 = (bf16[16,512]{1,0:T(8,128)(2,1)}, f32[16,512]{1,0:T(8,128)}, f32[16,512]{1,0:T(8,128)}) custom-call(bf16[16,2048]{1,0:T(8,128)(2,1)} %bitcast.13, s32[10,1,1024]{2,1,0:T(1,128)} %bitcast.14, bf16[16,512]{1,0:T(8,128)(2,1)} %w1s_in.1, bf16[16,512]{1,0:T(8,128)(2,1)} %w1n_in.1, bf16[512,512]{1,0:T(8,128)(2,1)} %w2s_in.1, ...), custom_call_target="tpu_custom_call" | custom-call | tf_op jit(solution)/shard_map/pallas_call | solution.py:523
  78.2 0.0 copy-start.1
  78.2 1.3 %copy.16 = bf16[1,1,16,512]{3,2,1,0:T(8,128)(2,1)} copy(bf16[1,1,16,512]{3,2,1,0:T(8,128)(2,1)} %bitcast.18) | data formatting | bytes 32768
  79.5 0.0 copy-done.1
  79.5 0.0 copy-start
  79.5 0.6 copy.17
  80.1 0.2 copy-done
  80.3 0.6 copy.18
Async XLA Ops:
  78.2 1.3 %copy-start.1 = (f32[16,512]{1,0:T(8,128)S(1)}, f32[16,512]{1,0:T(8,128)}, u32[]{:S(2)}) copy-start(f32[16,512]{1,0:T(8,128)} %get-tuple-element.7) | copy-start | bytes 98308
  79.5 0.8 copy-start

commit v6 on v5

--- a/solution.py
+++ b/solution.py
@@ -17,9 +17,11 @@
 BF16 = jnp.bfloat16
 
 WINDOW_PLAN = (
-    (0, (5, -5, -8, 2, -2, 1, -1)),
-    (5, (2, -2, 1, -1)),
-    (-5, (2, -2, 1, -1)),
+    (0, (3, -3, 1, -1)),
+    (3, (-3, 1, -1)),
+    (-3, (3, 1, -1)),
+    (6, (-2, 1, -1)),
+    (-6, (1, -1)),
 )
 
 

time: 81.2 us -> 77.2 us (0.951)
  Pallas kernels: 77.5 us -> 73.5 us
    pallas_call x1, Pallas kernels: 77.5 us -> 73.5 us  [on_device(): pl.pallas_call(kernel, out_shape=(jax.ShapeDtypeStruct((16, 512), BF16),...]
where the time goes in v6:
time: 77.2 us; the launch traced here: 76.9 us
  Pallas kernels  73.5 us (95%)
  local copies, waits for them, and re-layouts  2.72 us (4%)
    pallas_call x1, Pallas kernels, on_device(): pl.pallas_call(kernel, out_shape=(jax.ShapeDtypeStruct((16, 512), BF16),...  73.5 us
    unnamed x7, local copies, waits for them, and re-layouts  2.72 us

profile of v6, /device:TPU:1, one launch (start us, length us, event | category | flops | bytes accessed | tf_op | source)
XLA Modules:
  0.0 76.9 jit_solution(851087071552751853)
XLA Ops:
  0.6 73.5 %shard_map.121 = (bf16[16,512]{1,0:T(8,128)(2,1)}, f32[16,512]{1,0:T(8,128)}, f32[16,512]{1,0:T(8,128)}) custom-call(bf16[16,2048]{1,0:T(8,128)(2,1)} %bitcast.13, s32[10,1,1024]{2,1,0:T(1,128)} %bitcast.14, bf16[16,512]{1,0:T(8,128)(2,1)} %w1s_in.1, bf16[16,512]{1,0:T(8,128)(2,1)} %w1n_in.1, bf16[512,512]{1,0:T(8,128)(2,1)} %w2s_in.1, ...), custom_call_target="tpu_custom_call" | custom-call | tf_op jit(solution)/shard_map/pallas_call | solution.py:525
  74.2 0.0 copy-start.1
  74.2 1.3 %copy.16 = bf16[1,1,16,512]{3,2,1,0:T(8,128)(2,1)} copy(bf16[1,1,16,512]{3,2,1,0:T(8,128)(2,1)} %bitcast.18) | data formatting | bytes 32768
  75.5 0.0 copy-done.1
  75.5 0.0 copy-start
  75.5 0.6 copy.17
  76.1 0.2 copy-done
  76.3 0.6 copy.18
Async XLA Ops:
  74.2 1.3 %copy-start.1 = (f32[16,512]{1,0:T(8,128)S(1)}, f32[16,512]{1,0:T(8,128)}, u32[]{:S(2)}) copy-start(f32[16,512]{1,0:T(8,128)} %get-tuple-element.7) | copy-start | bytes 98308
  75.5 0.8 %copy-start = (f32[16,512]{1,0:T(8,128)S(1)}, f32[16,512]{1,0:T(8,128)}, u32[]{:S(2)}) copy-start(f32[16,512]{1,0:T(8,128)} %get-tuple-element.8) | copy-start | bytes 98308
